TPU v7x, 32 devices: a whole 2x2x4 slice. The times are simulated.
32 devices in a mesh: side: 2 (over core), row: 4 (over y, x), col: 4 (over z).
Axes of the slice: x: 2, y: 2, z: 4, core: 2. Of those that a mesh axis runs over, the one named last changes fastest.
Arguments:
- right_side: float32 [256, 128, 548], P('row', 'col', 'side'), may hold values from -24 to 24
- couplings: float32 [4, 256, 128], P(None, 'row', 'col'), may hold values from 0.04 to 0.2
- channel_rates: float32 [548], P('side'), may hold values from 0.2 to 1
- weight_in: float32 [548, 1024], replicated, may hold values from -0.25 to 0.25
- weight_mid: float32 [1024, 1024], replicated, may hold values from -0.1875 to 0.1875
- weight_out: float32 [1024, 616], replicated, may hold values from -0.1875 to 0.1875
- inverse_cov: float32 [616, 616], replicated, may hold values from -2 to 8, as said below
- profile_cells: int32 [2, 8192], P(None, ('row', 'col')), may hold values from 0 to 2047
- profile_counts: int32 [32], replicated, may hold values from 1 to 512, 4096 in all
- gate_first: bfloat16 [16384, 1024], P(('side', 'row', 'col')), may hold values from 0 to 1.09375
- gate_second: bfloat16 [16384, 1024], P(('side', 'row', 'col')), may hold values from 0 to 1.09375
Outputs:
- solution: float32 [256, 128, 548], P('row', 'col', 'side')
- residual: float32 [256, 128, 548], P('row', 'col', 'side')
Inputs may be any that keep to these rules, and one draw needn't show every extreme that they name: `profile_counts`: entry d counts the live profiles of device d in the order side, row, col; they fill its first slots. The entries add up to 4096, and the largest is 512. `profile_cells`: entry [s, t * 512 + i] is the cell, numbered latitude-major within tile t, observed by slot i of device s * 16 + t; entries of slots that are not live are unused. `inverse_cov`: symmetric positive definite.
All inputs are finite; a program needn't handle non-finite values.
Results may differ from a plain program's by a relative error of at most 0.0003.
Values may be sent and summed in bfloat16 or wider, within the bound.
A program may use at most 128 MiB of HBM per device.

v0:
```python
import functools

import jax
import jax.numpy as jnp
from jax import lax
from jax.experimental import pallas as pl
from jax.experimental.pallas import tpu as pltpu
from jax.sharding import PartitionSpec as P

MESH = pl.DeviceIdType.MESH


def sums_kernel(sides, rows, cols, x_ref, o_ref, plane, line, send_sem, recv_sem):
    side, row, col = lax.axis_index("side"), lax.axis_index("row"), lax.axis_index("col")
    near = [
        (lax.rem(side + ds, sides), lax.rem(row + dr, rows), col)
        for ds in range(sides)
        for dr in range(rows)
        if ds + dr
    ]
    far = [(side, row, lax.rem(col + dc, cols)) for dc in range(1, cols)]
    barrier = pltpu.get_barrier_semaphore()
    for peer in near + far:
        pl.semaphore_signal(barrier, inc=1, device_id=peer, device_id_type=MESH)
    pl.semaphore_wait(barrier, len(near) + len(far))

    def exchange(value, peers, buffer, slot, first):
        buffer[slot] = value
        copies = [
            pltpu.make_async_remote_copy(
                src_ref=buffer.at[slot],
                dst_ref=buffer.at[slot],
                send_sem=send_sem.at[first + k],
                recv_sem=recv_sem.at[first + k],
                device_id=peer,
                device_id_type=MESH,
            )
            for k, peer in enumerate(peers)
        ]
        for copy in copies:
            copy.start()
        for copy in copies:
            copy.wait()
        return jnp.sum(buffer[...], axis=0)

    plane_sum = exchange(x_ref[...], near, plane, side * rows + row, 0)
    o_ref[...] = exchange(plane_sum, far, line, col, len(near))


VMEM = pl.BlockSpec(memory_space=pltpu.VMEM)
SMEM = pl.BlockSpec(memory_space=pltpu.SMEM)
LANES = 128
GRANT = 56 * 1024 * 1024


def call(kernel, shapes, specs, scratch, *operands, **params):
    out = [jax.ShapeDtypeStruct(shape, jnp.float32) for shape in shapes]
    params = pltpu.CompilerParams(vmem_limit_bytes=GRANT, **params)
    return pl.pallas_call(
        kernel,
        out_shape=out,
        in_specs=specs,
        out_specs=[VMEM] * len(out),
        scratch_shapes=scratch,
        compiler_params=params,
    )(*operands)


def all_sums(block):
    sides, rows, cols = (lax.axis_size(axis) for axis in ("side", "row", "col"))
    count = sides * rows - 1 + cols - 1
    scratch = [
        pltpu.VMEM((sides * rows, *block.shape), jnp.float32),
        pltpu.VMEM((cols, *block.shape), jnp.float32),
        pltpu.SemaphoreType.DMA((count,)),
        pltpu.SemaphoreType.DMA((count,)),
    ]
    kernel = functools.partial(sums_kernel, sides, rows, cols)
    return call(kernel, [block.shape], [VMEM], scratch, block, collective_id=0, has_side_effects=True)[0]


def halo_kernel(rows, cols, first_lat, last_lat, first_lon, last_lon, *rest):
    outs, lands, (send_sem, recv_sem) = rest[:4], rest[4:8], rest[8:]
    side, row, col = lax.axis_index("side"), lax.axis_index("row"), lax.axis_index("col")
    below = (side, lax.rem(row + rows - 1, rows), col)
    above = (side, lax.rem(row + 1, rows), col)
    behind = (side, row, lax.rem(col + cols - 1, cols))
    ahead = (side, row, lax.rem(col + 1, cols))
    peers = (above, below, ahead, behind)
    barrier = pltpu.get_barrier_semaphore()
    for peer in peers:
        pl.semaphore_signal(barrier, inc=1, device_id=peer, device_id_type=MESH)
    pl.semaphore_wait(barrier, 4)
    copies = [
        pltpu.make_async_remote_copy(
            src_ref=source,
            dst_ref=land,
            send_sem=send_sem.at[k],
            recv_sem=recv_sem.at[k],
            device_id=peer,
            device_id_type=MESH,
        )
        for k, (source, land, peer) in enumerate(zip((last_lat, first_lat, last_lon, first_lon), lands, peers))
    ]
    for copy in copies:
        copy.start()
    for copy, land, out in zip(copies, lands, outs):
        copy.wait()
        out[...] = land[...]


def halos(first_lat, last_lat, first_lon, last_lon):
    kernel = functools.partial(halo_kernel, lax.axis_size("row"), lax.axis_size("col"))
    shapes = [first_lat.shape, first_lat.shape, first_lon.shape, first_lon.shape]
    scratch = [pltpu.VMEM(shape, jnp.float32) for shape in shapes]
    scratch += [pltpu.SemaphoreType.DMA((4,)), pltpu.SemaphoreType.DMA((4,))]
    operands = (first_lat, last_lat, first_lon, last_lon)
    return call(kernel, shapes, [VMEM] * 4, scratch, *operands, collective_id=1, has_side_effects=True)


def live_counts(counts):
    side = lax.axis_index("side")
    tiles = lax.axis_size("row") * lax.axis_size("col")
    tile = lax.axis_index("row") * lax.axis_size("col") + lax.axis_index("col")
    return (side, counts[side * tiles + tile]), (1 - side, counts[(1 - side) * tiles + tile])


def gather_kernel(field, before, after, left, right, weights, rates, cells, counts, own, other, image):
    lats, lons, width = field.shape
    rate = rates[...]
    whole = width // LANES * LANES
    image[:, whole:] = jnp.zeros((image.shape[0], image.shape[1] - whole), jnp.float32)

    def line(i, value, following, preceding):
        weight = weights[i]
        east = jnp.concatenate([value[1:], right[pl.ds(i, 1)]], axis=0)
        west = jnp.concatenate([left[pl.ds(i, 1)], value[:-1]], axis=0)
        flux = weight[:, 0:1] * (east - value) + weight[:, 1:2] * (west - value)
        flux = flux + weight[:, 2:3] * (following - value) + weight[:, 3:4] * (preceding - value)
        image[pl.ds(pl.multiple_of(i * lons, lons), lons), :width] = value + rate * flux

    line(0, field[0], field[1], before[...])
    line(lats - 1, field[lats - 1], after[...], field[lats - 2])

    @pl.loop(1, lats - 1)
    def _(i):
        line(i, field[i], field[i + 1], field[i - 1])

    for (side, live), out in zip(live_counts(counts), (own, other)):

        @pl.loop(0, (live + 7) // 8)
        def _(j):
            base = pl.multiple_of(j * 8, 8)
            lines = [image[pl.ds(cells[side, base + k], 1)] for k in range(8)]
            out[pl.ds(base, 8)] = jnp.concatenate(lines, axis=0)


def scatter_kernel(own, other, weights, rates, cells, counts, spread, to_before, to_after, to_left, to_right):
    lats, lons, _ = weights.shape
    width = rates.shape[1]
    rate = rates[...]
    spread[...] = jnp.zeros_like(spread)
    for (side, live), grads in zip(live_counts(counts), (own, other)):

        @pl.loop(0, live)
        def _(i):
            cell = cells[side, i]
            spread[pl.ds(cell, 1)] = spread[pl.ds(cell, 1)] + grads[pl.ds(i, 1)]

    to_before[...] = weights[0][:, 3:4] * (rate * spread[:lons, :width])
    to_after[...] = weights[lats - 1][:, 2:3] * (rate * spread[(lats - 1) * lons :, :width])

    @pl.loop(0, lats)
    def _(i):
        base = pl.multiple_of(i * lons, lons)
        weight = weights[i]
        lines = rate * spread[pl.ds(base, lons), :width]
        to_left[pl.ds(i, 1)] = weight[:1, 1:2] * lines[:1]
        to_right[pl.ds(i, 1)] = weight[lons - 1 :, 0:1] * lines[lons - 1 :]


def adjoint_kernel(is_first, spread, before, after, left, right, weights, rates, field, sums, out, *rest):
    lats, lons, width = field.shape
    rate = rates[...]

    def scaled(i):
        return rate * spread[pl.ds(pl.multiple_of(i * lons, lons), lons), :width]

    def line(i, preceding, following, totals):
        weight = weights[i]
        value = spread[pl.ds(pl.multiple_of(i * lons, lons), lons), :width]
        flow = rate * value
        east = weight[:, 0:1] * flow
        west = weight[:, 1:2] * flow
        total = weight[:, 0:1] + weight[:, 1:2] + weight[:, 2:3] + weight[:, 3:4]
        result = value - total * flow + preceding + following
        result = result + jnp.concatenate([left[pl.ds(i, 1)], east[:-1]], axis=0)
        result = result + jnp.concatenate([west[1:], right[pl.ds(i, 1)]], axis=0)
        out[i] = result
        known = field[i]
        if not is_first:
            return (totals[0] + known * result,)
        rest[2][pl.ds(i, 1)] = result[:1]
        rest[3][pl.ds(i, 1)] = result[lons - 1 :]
        return totals[0] + known * known, totals[1] + known * result, totals[2] + result * result

    def inner(i, totals):
        return line(i, weights[i - 1][:, 2:3] * scaled(i - 1), weights[i + 1][:, 3:4] * scaled(i + 1), totals)

    totals = tuple(jnp.zeros((lons, width), jnp.float32) for _ in range(3 if is_first else 1))
    totals = line(0, before[...], weights[1][:, 3:4] * scaled(1), totals)
    totals = lax.fori_loop(1, lats - 1, inner, totals)
    totals = line(lats - 1, weights[lats - 2][:, 2:3] * scaled(lats - 2), after[...], totals)
    lines = lax.broadcasted_iota(jnp.int32, sums.shape, 0)
    block = sums[...]
    for k, total in enumerate(totals):
        block = jnp.where(lines == (k if is_first else 3), jnp.sum(total), block)
    if is_first:
        rest[0][...] = out[0]
        rest[1][...] = out[lats - 1]
    rest[-1][...] = block


def network_kernel(own, other, gate_one, gate_two, w_own, w_other, w_mid, w_out, cov, counts, d_own, d_other, scale_out, *scratch):
    pairs = [scratch[2 * k : 2 * k + 2] for k in range(5)]
    squares = []
    for full, (high, low) in zip((w_own, w_other, w_mid, w_out, cov), pairs):
        chunk = 32

        def split(c, total, full=full, high=high, low=low):
            lines = pl.ds(pl.multiple_of(c * chunk, chunk), chunk)
            value = full[lines]
            rounded = value.astype(jnp.bfloat16)
            high[lines] = rounded
            low[lines] = (value - rounded.astype(jnp.float32)).astype(jnp.bfloat16)
            return total + value * value

        start = jnp.zeros((chunk, full.shape[1]), jnp.float32)
        squares.append(jnp.sum(lax.fori_loop(0, full.shape[0] // chunk, split, start), axis=(0, 1), keepdims=True))
    bound = (squares[0] + squares[1]) * squares[2] * squares[3] * jnp.sqrt(squares[4])
    scale = 1.0 / jnp.maximum(bound, 1.0)
    scale_out[...] = jnp.broadcast_to(scale, scale_out.shape)
    p_own, p_other, p_mid, p_out, p_cov = pairs

    def product(value, pair, back=False):
        dims = (((1,), (1 if back else 0,)), ((), ()))
        high = value.astype(jnp.bfloat16)
        low = (value - high.astype(jnp.float32)).astype(jnp.bfloat16)

        def dot(left, right):
            return lax.dot_general(left, right[...], dims, preferred_element_type=jnp.float32)

        return dot(high, pair[0]) + (dot(low, pair[0]) + dot(high, pair[1]))

    rows = min(256, own.shape[0])
    live = live_counts(counts)[0][1]

    @pl.loop(0, (live + rows - 1) // rows)
    def _(j):
        lines = pl.ds(pl.multiple_of(j * rows, rows), rows)
        g1 = gate_one[lines].astype(jnp.float32)
        hidden = (product(own[lines], p_own) + product(other[lines], p_other)) * g1
        hidden = product(hidden, p_mid) * gate_two[lines].astype(jnp.float32)
        weighted = product(product(hidden, p_out), p_cov) * scale
        back = product(weighted, p_out, True) * gate_two[lines].astype(jnp.float32)
        back = product(back, p_mid, True) * gate_one[lines].astype(jnp.float32)
        d_own[lines] = product(back, p_own, True)
        d_other[lines] = product(back, p_other, True)


def combination(scale, bb, bw, ww, wx):
    bw = bw / scale
    curve = bb + bw
    step = bb / curve
    rest = bw / curve
    grown = step / scale
    ratio = (grown * ww / bb) * grown - rest * rest
    norm = ratio * bb
    along = norm + rest * rest * bw - 2.0 * rest * (grown * ww / scale) + grown * (grown * wx) / scale
    second = norm / (along - ratio * norm / step)
    mixed = rest + ratio
    of_solution = (step + second * mixed, -second * grown)
    of_residual = (
        rest - second * mixed,
        -grown - second * (mixed / scale - grown),
        (second / scale) * grown,
    )
    return of_solution, of_residual


def finish_kernel(sums, scale, b, w, x, solution, residual):
    values = [sums[k : k + 1, 0:1] for k in range(4)]
    of_solution, of_residual = combination(scale[0:1, 0:1], *values)
    solution[...] = of_solution[0] * b[...] + of_solution[1] * w[...]
    residual[...] = of_residual[0] * b[...] + of_residual[1] * w[...] + of_residual[2] * x[...]


def finish(sums, scale, b, w, x):
    lats, lons, width = b.shape
    part = 8 if lats % 8 == 0 else lats
    whole = pl.BlockSpec(sums.shape, lambda i: (0, 0))
    block = pl.BlockSpec((part, lons, width), lambda i: (i, 0, 0))
    return pl.pallas_call(
        finish_kernel,
        grid=(lats // part,),
        out_shape=[jax.ShapeDtypeStruct(b.shape, jnp.float32)] * 2,
        in_specs=[whole, whole, block, block, block],
        out_specs=[block, block],
        compiler_params=pltpu.CompilerParams(vmem_limit_bytes=GRANT),
    )(sums, scale, b, w, x)


def swapped(value):
    return lax.ppermute(value, "side", [(0, 1), (1, 0)])


def padded(array, rows, columns):
    return jnp.pad(array, ((0, rows - array.shape[0]), (0, columns - array.shape[1])))


def local(
    right_side,
    couplings,
    channel_rates,
    weight_in,
    weight_mid,
    weight_out,
    inverse_cov,
    profile_cells,
    profile_counts,
    gate_first,
    gate_second,
):
    side = lax.axis_index("side")
    lats, lons, width = right_side.shape
    slots = profile_cells.shape[1]
    wide = -(-width // LANES) * LANES
    channels = -(-weight_out.shape[1] // LANES) * LANES
    latitude = lax.axis_index("row") * lats + jnp.arange(lats)
    north_open = (latitude < lats * lax.axis_size("row") - 1)[:, None]
    south_open = (latitude > 0)[:, None]
    weights = jnp.stack(
        [
            couplings[0],
            couplings[1],
            jnp.where(north_open, couplings[2], 0.0),
            jnp.where(south_open, couplings[3], 0.0),
        ],
        axis=2,
    )
    rates = channel_rates.reshape(1, width)
    halves = [lax.dynamic_slice_in_dim(weight_in, part * width, width, 0) for part in (side, 1 - side)]
    matrices = [padded(half, wide, half.shape[1]) for half in halves]
    matrices += [weight_mid, padded(weight_out, weight_out.shape[0], channels), padded(inverse_cov, channels, channels)]
    split_scratch = [pltpu.VMEM(matrix.shape, jnp.bfloat16) for matrix in matrices for _ in range(2)]
    lat_edge, lon_edge = (lons, width), (lats, width)

    def spread(field, edges, known, sums, is_first):
        around = halos(*edges)
        image = [pltpu.VMEM((lats * lons, wide), jnp.float32)]
        specs = [VMEM] * 7 + [SMEM] * 2
        operands = (field, *around, weights, rates, profile_cells, profile_counts)
        own, other = call(gather_kernel, [(slots, wide)] * 2, specs, image, *operands)
        other = swapped(other)
        operands = (own, other, gate_first, gate_second, *matrices, profile_counts)
        shapes = [(slots, wide)] * 2 + [(8, LANES)]
        own, other, scale = call(network_kernel, shapes, [VMEM] * 9 + [SMEM], split_scratch, *operands)
        other = swapped(other)
        shapes = [(lats * lons, wide), lat_edge, lat_edge, lon_edge, lon_edge]
        operands = (own, other, weights, rates, profile_cells, profile_counts)
        summed, *edges = call(scatter_kernel, shapes, [VMEM] * 4 + [SMEM] * 2, [], *operands)
        around = halos(*edges)
        shapes = [field.shape] + ([lat_edge, lat_edge, lon_edge, lon_edge] if is_first else []) + [(8, LANES)]
        operands = (summed, *around, weights, rates, known, sums)
        out, *edges, sums = call(functools.partial(adjoint_kernel, is_first), shapes, [VMEM] * 9, [], *operands)
        return out, edges, sums, scale

    edges = (right_side[0], right_side[lats - 1], right_side[:, 0], right_side[:, lons - 1])
    first, edges, sums, scale = spread(right_side, edges, right_side, jnp.zeros((8, LANES), jnp.float32), True)
    second, _, sums, _ = spread(first, edges, first, sums, False)
    return tuple(finish(all_sums(sums), scale, right_side, first, second))


def solution(mesh):
    in_specs = (
        P("row", "col", "side"),
        P(None, "row", "col"),
        P("side"),
        P(),
        P(),
        P(),
        P(),
        P(None, ("row", "col")),
        P(),
        P(("side", "row", "col"), None),
        P(("side", "row", "col"), None),
    )
    out_specs = (P("row", "col", "side"), P("row", "col", "side"))
    return jax.shard_map(local, mesh=mesh, in_specs=in_specs, out_specs=out_specs, check_vma=False)
```

profile of v0, /device:TPU:0, one launch (start us, length us, event | category | flops | bytes accessed | tf_op | source)
XLA Modules:
  0.0 237.5 jit_solution(2002468858556624906)
XLA Ops:
  0.6 1.5 slice_bitcast_fusion
  2.1 1.5 fusion.2
  6.3 1.9 copy.29.weights
  8.9 12.9 %shard_map.122 = (f32[32,274]{1,0:T(8,128)}, f32[32,274]{1,0:T(8,128)}, f32[64,274]{1,0:T(8,128)}, f32[64,274]{1,0:T(8,128)}) custom-call(f32[32,274]{1,0:T(8,128)} %get-tuple-element.91.first_lat, f32[32,274]{1,0:T(8,128)} %get-tuple-element.90.last_lat, f32[64,274]{1,0:T(8,128)} %get-tuple-element.99.first_lon, f32[64,274]{1,0:T(8,128)} %get-tuple-element.98.last_lon), custom_call_target="tpu_custom_call" | custom-call | tf_op jit(solution)/shard_map/pallas_call | solution.py:59
  21.8 10.8 %shard_map.123 = (f32[512,384]{1,0:T(8,128)}, f32[512,384]{1,0:T(8,128)}) custom-call(f32[64,32,274]{2,1,0:T(8,128)} %b.1, f32[32,274]{1,0:T(8,128)} %get-tuple-element.45.before, f32[32,274]{1,0:T(8,128)} %get-tuple-element.46.after, f32[64,274]{1,0:T(8,128)} %get-tuple-element.47.left, f32[64,274]{1,0:T(8,128)} %get-tuple-element.48.right, ...), custom_call_target="tpu_custom_call" | custom-call | tf_op jit(solution)/shard_map/pallas_call | solution.py:59
  32.6 2.9 %pad.18.cov = f32[640,640]{1,0:T(8,128)} pad(f32[616,616]{1,0:T(8,128)} %param.17, f32[]{:T(128)} %constant.8.clone.1), padding=0_24x0_24 | pad | bytes 3156228 | tf_op jit(solution)/shard_map/jit(_pad)/pad | solution.py:318
  37.1 1.4 pad.15.w_own
  38.5 2.1 copy.30
  40.7 1.7 pad.17.w_out
  43.2 20.4 %shard_map.124 = (f32[512,384]{1,0:T(8,128)}, f32[512,384]{1,0:T(8,128)}, f32[8,128]{1,0:T(8,128)}) custom-call(f32[512,384]{1,0:T(8,128)} %get-tuple-element.49.own, f32[512,384]{1,0:T(8,128)} %copy-done.1, bf16[512,1024]{1,0:T(8,128)(2,1)} %gate_one.3, bf16[512,1024]{1,0:T(8,128)(2,1)} %gate_two.3, f32[384,1024]{1,0:T(8,128)} %pad.15.w_own, ...), custom_call_target="tpu_custom_call" | custom-call | tf_op jit(solution)/shard_map/pallas_call | solution.py:59
  64.0 2.2 collective-permute-done.1.other
  67.1 11.8 %shard_map.125 = (f32[2048,384]{1,0:T(8,128)}, f32[32,274]{1,0:T(8,128)}, f32[32,274]{1,0:T(8,128)}, f32[64,274]{1,0:T(8,128)}, f32[64,274]{1,0:T(8,128)}) custom-call(f32[512,384]{1,0:T(8,128)} %get-tuple-element.51.own, f32[512,384]{1,0:T(8,128)} %copy-done.4, f32[64,32,4]{2,1,0:T(8,128)} %copy.29.weights, f32[1,274]{1,0:T(1,128)} %reshape.77.rates, ...), custom_call_target="tpu_custom_call" | custom-call | tf_op jit(solution)/shard_map/pallas_call | solution.py:59
  78.8 22.4 %shard_map.126 = (f32[32,274]{1,0:T(8,128)}, f32[32,274]{1,0:T(8,128)}, f32[64,274]{1,0:T(8,128)}, f32[64,274]{1,0:T(8,128)}) custom-call(f32[32,274]{1,0:T(8,128)} %get-tuple-element.54.first_lat, f32[32,274]{1,0:T(8,128)} %get-tuple-element.55.last_lat, f32[64,274]{1,0:T(8,128)} %get-tuple-element.56.first_lon, f32[64,274]{1,0:T(8,128)} %get-tuple-element.57.last_lon), custom_call_target="tpu_custom_call" | custom-call | tf_op jit(solution)/shard_map/pallas_call | solution.py:59
  101.8 15.9 %shard_map.127 = (f32[64,32,274]{2,1,0:T(8,128)}, f32[32,274]{1,0:T(8,128)}, f32[32,274]{1,0:T(8,128)}, f32[64,274]{1,0:T(8,128)}, f32[64,274]{1,0:T(8,128)}, /*index=5*/f32[8,128]{1,0:T(8,128)}) custom-call(f32[2048,384]{1,0:T(8,128)} %get-tuple-element.53.spread, f32[32,274]{1,0:T(8,128)} %get-tuple-element.58.before, f32[32,274]{1,0:T(8,128)} %get-tuple-element.59.after, ...), custom_call_target="tpu_custom_call" | custom-call | tf_op jit(solution)/shard_map/pallas_call | solution.py:59
  117.7 9.9 %shard_map.128 = (f32[32,274]{1,0:T(8,128)}, f32[32,274]{1,0:T(8,128)}, f32[64,274]{1,0:T(8,128)}, f32[64,274]{1,0:T(8,128)}) custom-call(f32[32,274]{1,0:T(8,128)} %get-tuple-element.63.first_lat, f32[32,274]{1,0:T(8,128)} %get-tuple-element.64.last_lat, f32[64,274]{1,0:T(8,128)} %get-tuple-element.65.first_lon, f32[64,274]{1,0:T(8,128)} %get-tuple-element.66.last_lon), custom_call_target="tpu_custom_call" | custom-call | tf_op jit(solution)/shard_map/pallas_call | solution.py:59
  127.7 10.8 %shard_map.129 = (f32[512,384]{1,0:T(8,128)}, f32[512,384]{1,0:T(8,128)}) custom-call(f32[64,32,274]{2,1,0:T(8,128)} %get-tuple-element.62.field.w, f32[32,274]{1,0:T(8,128)} %get-tuple-element.67.before, f32[32,274]{1,0:T(8,128)} %get-tuple-element.68.after, f32[64,274]{1,0:T(8,128)} %get-tuple-element.69.left, f32[64,274]{1,0:T(8,128)} %get-tuple-element.70.right, ...), custom_call_target="tpu_custom_call" | custom-call | tf_op jit(solution)/shard_map/pallas_call | solution.py:59
  138.5 2.5 %collective-permute-done.2.other = f32[512,384]{1,0:T(8,128)S(1)} collective-permute-done((f32[512,384]{1,0:T(8,128)}, f32[512,384]{1,0:T(8,128)S(1)}, u32[]{:S(2)}, u32[]{:S(2)}) %collective-permute-start.2) | collective-permute-done | bytes 786464 | tf_op jit(solution)/shard_map/ppermute | solution.py:314
  141.9 20.4 %shard_map.130 = (f32[512,384]{1,0:T(8,128)}, f32[512,384]{1,0:T(8,128)}, f32[8,128]{1,0:T(8,128)}) custom-call(f32[512,384]{1,0:T(8,128)} %get-tuple-element.71.own, f32[512,384]{1,0:T(8,128)} %copy-done.2, bf16[512,1024]{1,0:T(8,128)(2,1)} %gate_one.3, bf16[512,1024]{1,0:T(8,128)(2,1)} %gate_two.3, f32[384,1024]{1,0:T(8,128)} %pad.15.w_own, ...), custom_call_target="tpu_custom_call" | custom-call | tf_op jit(solution)/shard_map/pallas_call | solution.py:59
  162.4 2.4 collective-permute-done.3.other
  165.7 11.6 %shard_map.131 = (f32[2048,384]{1,0:T(8,128)}, f32[32,274]{1,0:T(8,128)}, f32[32,274]{1,0:T(8,128)}, f32[64,274]{1,0:T(8,128)}, f32[64,274]{1,0:T(8,128)}) custom-call(f32[512,384]{1,0:T(8,128)} %get-tuple-element.73.own, f32[512,384]{1,0:T(8,128)} %copy-done.3, f32[64,32,4]{2,1,0:T(8,128)} %copy.29.weights, f32[1,274]{1,0:T(1,128)} %reshape.77.rates, ...), custom_call_target="tpu_custom_call" | custom-call | tf_op jit(solution)/shard_map/pallas_call | solution.py:59
  177.2 24.0 %shard_map.132 = (f32[32,274]{1,0:T(8,128)}, f32[32,274]{1,0:T(8,128)}, f32[64,274]{1,0:T(8,128)}, f32[64,274]{1,0:T(8,128)}) custom-call(f32[32,274]{1,0:T(8,128)} %get-tuple-element.76.first_lat, f32[32,274]{1,0:T(8,128)} %get-tuple-element.77.last_lat, f32[64,274]{1,0:T(8,128)} %get-tuple-element.78.first_lon, f32[64,274]{1,0:T(8,128)} %get-tuple-element.79.last_lon), custom_call_target="tpu_custom_call" | custom-call | tf_op jit(solution)/shard_map/pallas_call | solution.py:59
  201.2 15.6 %shard_map.133 = (f32[64,32,274]{2,1,0:T(8,128)}, f32[8,128]{1,0:T(8,128)}) custom-call(f32[2048,384]{1,0:T(8,128)} %get-tuple-element.75.spread, f32[32,274]{1,0:T(8,128)} %get-tuple-element.80.before, f32[32,274]{1,0:T(8,128)} %get-tuple-element.81.after, f32[64,274]{1,0:T(8,128)} %get-tuple-element.82.left, f32[64,274]{1,0:T(8,128)} %get-tuple-element.83.right, ...), custom_call_target="tpu_custom_call" | custom-call | tf_op jit(solution)/shard_map/pallas_call | solution.py:59
  216.9 11.9 %shard_map.134.sums = f32[8,128]{1,0:T(8,128)} custom-call(f32[8,128]{1,0:T(8,128)} %get-tuple-element.85.x_ref), custom_call_target="tpu_custom_call" | custom-call | tf_op jit(solution)/shard_map/pallas_call | solution.py:59
  228.8 8.7 %shard_map.135 = (f32[64,32,274]{2,1,0:T(8,128)}, f32[64,32,274]{2,1,0:T(8,128)}) custom-call(f32[8,128]{1,0:T(8,128)} %shard_map.134.sums, f32[8,128]{1,0:T(8,128)} %get-tuple-element.86.scale, f32[64,32,274]{2,1,0:T(8,128)} %b.1, f32[64,32,274]{2,1,0:T(8,128)} %get-tuple-element.62.field.w, f32[64,32,274]{2,1,0:T(8,128)} %get-tuple-element.87.x), custom_call_target="tpu_custom_call" | custom-call | tf_op jit(solution)/shard_map/pallas_call | solution.py:303
  (24 shorter events, 9.7 us)
Async XLA Ops:
  32.6 2.9 %copy-start = (f32[548,1024]{1,0:T(8,128)S(1)}, f32[548,1024]{1,0:T(8,128)}, u32[]{:S(2)}) copy-start(f32[548,1024]{1,0:T(8,128)} %param.14) | copy-start | bytes 6733828
  32.6 9.7 %collective-permute-start = (f32[512,384]{1,0:T(8,128)}, f32[512,384]{1,0:T(8,128)S(1)}, u32[]{:S(2)}, u32[]{:S(2)}) collective-permute-start(f32[512,384]{1,0:T(8,128)} %get-tuple-element.50), channel_id=1, source_target_pairs={{0,16},{16,0},{1,17},{17,1},{2,18},{18,2},{3,19},{19,3},{4,20},{20... | collective-permute-start | bytes 2359304 | tf_op jit(solution)/shard_map/ppermute | solution.py:314
  42.3 0.9 copy-start.1
  63.6 2.5 %collective-permute-start.1 = (f32[512,384]{1,0:T(8,128)}, f32[512,384]{1,0:T(8,128)S(1)}, u32[]{:S(2)}, u32[]{:S(2)}) collective-permute-start(f32[512,384]{1,0:T(8,128)} %get-tuple-element.52), channel_id=1, source_target_pairs={{0,16},{16,0},{1,17},{17,1},{2,18},{18,2},{3,19},{19,3},{4,20},{20... | collective-permute-start | bytes 2359304 | tf_op jit(solution)/shard_map/ppermute | solution.py:314
  66.1 0.9 copy-start.4
  138.5 2.5 %collective-permute-start.2 = (f32[512,384]{1,0:T(8,128)}, f32[512,384]{1,0:T(8,128)S(1)}, u32[]{:S(2)}, u32[]{:S(2)}) collective-permute-start(f32[512,384]{1,0:T(8,128)} %get-tuple-element.72), channel_id=1, source_target_pairs={{0,16},{16,0},{1,17},{17,1},{2,18},{18,2},{3,19},{19,3},{4,20},{20... | collective-permute-start | bytes 2359304 | tf_op jit(solution)/shard_map/ppermute | solution.py:314
  141.0 0.9 copy-start.2
  162.3 2.5 %collective-permute-start.3 = (f32[512,384]{1,0:T(8,128)}, f32[512,384]{1,0:T(8,128)S(1)}, u32[]{:S(2)}, u32[]{:S(2)}) collective-permute-start(f32[512,384]{1,0:T(8,128)} %get-tuple-element.74), channel_id=1, source_target_pairs={{0,16},{16,0},{1,17},{17,1},{2,18},{18,2},{3,19},{19,3},{4,20},{20... | collective-permute-start | bytes 2359304 | tf_op jit(solution)/shard_map/ppermute | solution.py:314
  164.8 0.9 copy-start.3
where the time goes:
time: 240 us; the launch traced here: 237 us
  Pallas kernels  207 us (86%)
  local copies, waits for them, and re-layouts  21.4 us (9%)
  waiting for transfers between devices  7.01 us (3%)
    pallas_call x13, Pallas kernels, call(): pl.pallas_call(kernel, out_shape=out, in_specs=specs, out_specs=[VMEM] *...  198 us
    pallas_call x1, Pallas kernels, finish(): pl.pallas_call(finish_kernel, grid=(lats // part,), out_shape=[jax.ShapeD...  8.66 us
    pad x4, local copies, waits for them, and re-layouts, padded(): jnp.pad(array, ((0, rows - array.shape[0]), (0, columns - array.shape[1])))  7.24 us
    ppermute x4, waiting for transfers between devices, swapped(): return lax.ppermute(value, 'side', [(0, 1), (1, 0)])  7.01 us
    unnamed x11, local copies, waits for them, and re-layouts  5.79 us
  transfers between devices with their start and end apart: 4, of which 3 were waited for; matrix products, arithmetic and copies ran while one was open for 4% of the time, Pallas kernels for 0%

commit v1 on v0

--- a/solution.py
+++ b/solution.py
@@ -50,12 +50,12 @@
 VMEM = pl.BlockSpec(memory_space=pltpu.VMEM)
 SMEM = pl.BlockSpec(memory_space=pltpu.SMEM)
 LANES = 128
-GRANT = 56 * 1024 * 1024
-
-
-def call(kernel, shapes, specs, scratch, *operands, **params):
+MIB = 1024 * 1024
+
+
+def call(kernel, grant, shapes, specs, scratch, *operands, **params):
     out = [jax.ShapeDtypeStruct(shape, jnp.float32) for shape in shapes]
-    params = pltpu.CompilerParams(vmem_limit_bytes=GRANT, **params)
+    params = pltpu.CompilerParams(vmem_limit_bytes=grant * MIB, **params)
     return pl.pallas_call(
         kernel,
         out_shape=out,
@@ -76,7 +76,7 @@
         pltpu.SemaphoreType.DMA((count,)),
     ]
     kernel = functools.partial(sums_kernel, sides, rows, cols)
-    return call(kernel, [block.shape], [VMEM], scratch, block, collective_id=0, has_side_effects=True)[0]
+    return call(kernel, 4, [block.shape], [VMEM], scratch, block, collective_id=0, has_side_effects=True)[0]
 
 
 def halo_kernel(rows, cols, first_lat, last_lat, first_lon, last_lon, *rest):
@@ -115,7 +115,7 @@
     scratch = [pltpu.VMEM(shape, jnp.float32) for shape in shapes]
     scratch += [pltpu.SemaphoreType.DMA((4,)), pltpu.SemaphoreType.DMA((4,))]
     operands = (first_lat, last_lat, first_lon, last_lon)
-    return call(kernel, shapes, [VMEM] * 4, scratch, *operands, collective_id=1, has_side_effects=True)
+    return call(kernel, 4, shapes, [VMEM] * 4, scratch, *operands, collective_id=1, has_side_effects=True)
 
 
 def live_counts(counts):
@@ -123,6 +123,20 @@
     tiles = lax.axis_size("row") * lax.axis_size("col")
     tile = lax.axis_index("row") * lax.axis_size("col") + lax.axis_index("col")
     return (side, counts[side * tiles + tile]), (1 - side, counts[(1 - side) * tiles + tile])
+
+
+def over_lines(lats, body, state):
+    steps = (lats - 2) // 4
+
+    def step(j, state):
+        for k in range(4):
+            state = body(1 + j * 4 + k, state)
+        return state
+
+    state = lax.fori_loop(0, steps, step, state)
+    for i in range(1 + steps * 4, lats - 1):
+        state = body(i, state)
+    return state
 
 
 def gather_kernel(field, before, after, left, right, weights, rates, cells, counts, own, other, image):
@@ -142,41 +156,62 @@
     line(0, field[0], field[1], before[...])
     line(lats - 1, field[lats - 1], after[...], field[lats - 2])
 
-    @pl.loop(1, lats - 1)
-    def _(i):
+    def inner(i, state):
         line(i, field[i], field[i + 1], field[i - 1])
+        return state
+
+    over_lines(lats, inner, 0)
 
     for (side, live), out in zip(live_counts(counts), (own, other)):
 
-        @pl.loop(0, (live + 7) // 8)
+        @pl.loop(0, (live + 15) // 16)
         def _(j):
-            base = pl.multiple_of(j * 8, 8)
-            lines = [image[pl.ds(cells[side, base + k], 1)] for k in range(8)]
-            out[pl.ds(base, 8)] = jnp.concatenate(lines, axis=0)
-
-
-def scatter_kernel(own, other, weights, rates, cells, counts, spread, to_before, to_after, to_left, to_right):
+            base = pl.multiple_of(j * 16, 16)
+            lines = [image[pl.ds(cells[side, base + k], 1)] for k in range(16)]
+            out[pl.ds(base, 16)] = jnp.concatenate(lines, axis=0)
+
+
+def scatter_kernel(own, other, weights, rates, cells, counts, spread, to_before, to_after, to_left, to_right, *parts):
     lats, lons, _ = weights.shape
     width = rates.shape[1]
     rate = rates[...]
-    spread[...] = jnp.zeros_like(spread)
+    for part in parts:
+        part[...] = jnp.zeros_like(part)
     for (side, live), grads in zip(live_counts(counts), (own, other)):
 
-        @pl.loop(0, live)
-        def _(i):
-            cell = cells[side, i]
-            spread[pl.ds(cell, 1)] = spread[pl.ds(cell, 1)] + grads[pl.ds(i, 1)]
+        @pl.loop(0, (live + len(parts) - 1) // len(parts))
+        def _(j):
+            base = j * len(parts)
+            places = [pl.ds(cells[side, base + k], 1) for k in range(len(parts))]
+            sums = []
+            for k, (part, place) in enumerate(zip(parts, places)):
+                term = jnp.where(base + k < live, grads[pl.ds(base + k, 1)], 0.0)
+                sums.append(part[place] + term)
+            for part, place, total in zip(parts, places, sums):
+                part[place] = total
+
+    block = 8 * lons
+
+    @pl.loop(0, spread.shape[0] // block)
+    def _(j):
+        lines = pl.ds(pl.multiple_of(j * block, block), block)
+        spread[lines] = (parts[0][lines] + parts[1][lines]) + (parts[2][lines] + parts[3][lines])
 
     to_before[...] = weights[0][:, 3:4] * (rate * spread[:lons, :width])
     to_after[...] = weights[lats - 1][:, 2:3] * (rate * spread[(lats - 1) * lons :, :width])
 
-    @pl.loop(0, lats)
-    def _(i):
-        base = pl.multiple_of(i * lons, lons)
-        weight = weights[i]
-        lines = rate * spread[pl.ds(base, lons), :width]
-        to_left[pl.ds(i, 1)] = weight[:1, 1:2] * lines[:1]
-        to_right[pl.ds(i, 1)] = weight[lons - 1 :, 0:1] * lines[lons - 1 :]
+    @pl.loop(0, lats // 8)
+    def _(j):
+        starts, ends = [], []
+        for k in range(8):
+            i = j * 8 + k
+            base = pl.multiple_of(i * lons, lons)
+            weight = weights[i]
+            starts.append(weight[:1, 1:2] * (rate * spread[pl.ds(base, 1), :width]))
+            ends.append(weight[lons - 1 :, 0:1] * (rate * spread[pl.ds(base + lons - 1, 1), :width]))
+        lines = pl.ds(pl.multiple_of(j * 8, 8), 8)
+        to_left[lines] = jnp.concatenate(starts, axis=0)
+        to_right[lines] = jnp.concatenate(ends, axis=0)
 
 
 def adjoint_kernel(is_first, spread, before, after, left, right, weights, rates, field, sums, out, *rest):
@@ -209,7 +244,7 @@
 
     totals = tuple(jnp.zeros((lons, width), jnp.float32) for _ in range(3 if is_first else 1))
     totals = line(0, before[...], weights[1][:, 3:4] * scaled(1), totals)
-    totals = lax.fori_loop(1, lats - 1, inner, totals)
+    totals = over_lines(lats, inner, totals)
     totals = line(lats - 1, weights[lats - 2][:, 2:3] * scaled(lats - 2), after[...], totals)
     lines = lax.broadcasted_iota(jnp.int32, sums.shape, 0)
     block = sums[...]
@@ -226,17 +261,28 @@
     squares = []
     for full, (high, low) in zip((w_own, w_other, w_mid, w_out, cov), pairs):
         chunk = 32
-
-        def split(c, total, full=full, high=high, low=low):
-            lines = pl.ds(pl.multiple_of(c * chunk, chunk), chunk)
-            value = full[lines]
+        rows, columns = full.shape
+
+        def store(start, value, high=high, low=low, columns=columns):
+            lines = pl.ds(start, chunk)
             rounded = value.astype(jnp.bfloat16)
-            high[lines] = rounded
-            low[lines] = (value - rounded.astype(jnp.float32)).astype(jnp.bfloat16)
-            return total + value * value
-
-        start = jnp.zeros((chunk, full.shape[1]), jnp.float32)
-        squares.append(jnp.sum(lax.fori_loop(0, full.shape[0] // chunk, split, start), axis=(0, 1), keepdims=True))
+            high[lines, :columns] = rounded
+            low[lines, :columns] = (value - rounded.astype(jnp.float32)).astype(jnp.bfloat16)
+            return value * value
+
+        def split(c, total, full=full, store=store):
+            start = pl.multiple_of(c * chunk, chunk)
+            return total + store(start, full[pl.ds(start, chunk)])
+
+        if high.shape != full.shape:
+            high[...] = jnp.zeros_like(high)
+            low[...] = jnp.zeros_like(low)
+        total = lax.fori_loop(0, rows // chunk, split, jnp.zeros((chunk, columns), jnp.float32))
+        left = rows % chunk
+        if left:
+            rest = jnp.concatenate([full[rows - left :], jnp.zeros((chunk - left, columns), jnp.float32)], axis=0)
+            total = total + store(rows - left, rest)
+        squares.append(jnp.sum(total, axis=(0, 1), keepdims=True))
     bound = (squares[0] + squares[1]) * squares[2] * squares[3] * jnp.sqrt(squares[4])
     scale = 1.0 / jnp.maximum(bound, 1.0)
     scale_out[...] = jnp.broadcast_to(scale, scale_out.shape)
@@ -261,8 +307,8 @@
         g1 = gate_one[lines].astype(jnp.float32)
         hidden = (product(own[lines], p_own) + product(other[lines], p_other)) * g1
         hidden = product(hidden, p_mid) * gate_two[lines].astype(jnp.float32)
-        weighted = product(product(hidden, p_out), p_cov) * scale
-        back = product(weighted, p_out, True) * gate_two[lines].astype(jnp.float32)
+        weighted = product(product(hidden, p_out, True), p_cov) * scale
+        back = product(weighted, p_out) * gate_two[lines].astype(jnp.float32)
         back = product(back, p_mid, True) * gate_one[lines].astype(jnp.float32)
         d_own[lines] = product(back, p_own, True)
         d_other[lines] = product(back, p_other, True)
@@ -306,16 +352,12 @@
         out_shape=[jax.ShapeDtypeStruct(b.shape, jnp.float32)] * 2,
         in_specs=[whole, whole, block, block, block],
         out_specs=[block, block],
-        compiler_params=pltpu.CompilerParams(vmem_limit_bytes=GRANT),
+        compiler_params=pltpu.CompilerParams(vmem_limit_bytes=24 * MIB),
     )(sums, scale, b, w, x)
 
 
 def swapped(value):
     return lax.ppermute(value, "side", [(0, 1), (1, 0)])
-
-
-def padded(array, rows, columns):
-    return jnp.pad(array, ((0, rows - array.shape[0]), (0, columns - array.shape[1])))
 
 
 def local(
@@ -350,9 +392,10 @@
     )
     rates = channel_rates.reshape(1, width)
     halves = [lax.dynamic_slice_in_dim(weight_in, part * width, width, 0) for part in (side, 1 - side)]
-    matrices = [padded(half, wide, half.shape[1]) for half in halves]
-    matrices += [weight_mid, padded(weight_out, weight_out.shape[0], channels), padded(inverse_cov, channels, channels)]
-    split_scratch = [pltpu.VMEM(matrix.shape, jnp.bfloat16) for matrix in matrices for _ in range(2)]
+    hidden = weight_in.shape[1]
+    matrices = [*halves, weight_mid, weight_out.T, inverse_cov]
+    shapes = [(wide, hidden), (wide, hidden), (hidden, hidden), (channels, hidden), (channels, channels)]
+    split_scratch = [pltpu.VMEM(shape, jnp.bfloat16) for shape in shapes for _ in range(2)]
     lat_edge, lon_edge = (lons, width), (lats, width)
 
     def spread(field, edges, known, sums, is_first):
@@ -360,19 +403,20 @@
         image = [pltpu.VMEM((lats * lons, wide), jnp.float32)]
         specs = [VMEM] * 7 + [SMEM] * 2
         operands = (field, *around, weights, rates, profile_cells, profile_counts)
-        own, other = call(gather_kernel, [(slots, wide)] * 2, specs, image, *operands)
+        own, other = call(gather_kernel, 16, [(slots, wide)] * 2, specs, image, *operands)
         other = swapped(other)
         operands = (own, other, gate_first, gate_second, *matrices, profile_counts)
         shapes = [(slots, wide)] * 2 + [(8, LANES)]
-        own, other, scale = call(network_kernel, shapes, [VMEM] * 9 + [SMEM], split_scratch, *operands)
+        own, other, scale = call(network_kernel, 46, shapes, [VMEM] * 9 + [SMEM], split_scratch, *operands)
         other = swapped(other)
+        parts = [pltpu.VMEM((lats * lons, wide), jnp.float32)] * 4
         shapes = [(lats * lons, wide), lat_edge, lat_edge, lon_edge, lon_edge]
         operands = (own, other, weights, rates, profile_cells, profile_counts)
-        summed, *edges = call(scatter_kernel, shapes, [VMEM] * 4 + [SMEM] * 2, [], *operands)
+        summed, *edges = call(scatter_kernel, 24, shapes, [VMEM] * 4 + [SMEM] * 2, parts, *operands)
         around = halos(*edges)
         shapes = [field.shape] + ([lat_edge, lat_edge, lon_edge, lon_edge] if is_first else []) + [(8, LANES)]
         operands = (summed, *around, weights, rates, known, sums)
-        out, *edges, sums = call(functools.partial(adjoint_kernel, is_first), shapes, [VMEM] * 9, [], *operands)
+        out, *edges, sums = call(functools.partial(adjoint_kernel, is_first), 16, shapes, [VMEM] * 9, [], *operands)
         return out, edges, sums, scale
 
     edges = (right_side[0], right_side[lats - 1], right_side[:, 0], right_side[:, lons - 1])

time: 240 us -> 186 us (0.78)
  Pallas kernels: 207 us -> 135 us
  starting transfers between devices: 0.49 us -> 29.8 us
  local copies, waits for them, and re-layouts: 21.4 us -> 12.2 us
    pallas_call x13, Pallas kernels: 198 us -> 131 us  [call(): pl.pallas_call(kernel, out_shape=out, in_specs=specs, out_specs=[VMEM] *...]
    ppermute x4, starting transfers between devices: 0.49 us -> 29.8 us  [swapped(): return lax.ppermute(value, 'side', [(0, 1), (1, 0)])]
    pad x4 -> x0, local copies, waits for them, and re-layouts: 7.24 us -> none  [padded(): jnp.pad(array, ((0, rows - array.shape[0]), (0, columns - array.shape[1])))]
    pallas_call x1, Pallas kernels: 8.66 us -> 4.51 us  [finish(): pl.pallas_call(finish_kernel, grid=(lats // part,), out_shape=[jax.ShapeD...]
    unnamed x11 -> x22, local copies, waits for them, and re-layouts: 5.79 us -> 5.35 us
  transfers between devices with their start and end apart: 4 -> 4, of which waited for: 3 -> 4; matrix products, arithmetic and copies ran while one was open for 4% -> 1% of each run, Pallas kernels for 0% -> 0%
where the time goes in v1:
time: 186 us
  Pallas kernels  135 us (73%)
  starting transfers between devices  29.8 us (16%)
  local copies, waits for them, and re-layouts  12.2 us (7%)
  waiting for transfers between devices  6.59 us (4%)
    pallas_call x13, Pallas kernels, call(): pl.pallas_call(kernel, out_shape=out, in_specs=specs, out_specs=[VMEM] *...  131 us
    ppermute x4, starting transfers between devices, swapped(): return lax.ppermute(value, 'side', [(0, 1), (1, 0)])  29.8 us
    ppermute x4, waiting for transfers between devices, swapped(): return lax.ppermute(value, 'side', [(0, 1), (1, 0)])  6.59 us
    unnamed x22, local copies, waits for them, and re-layouts  5.35 us
    pallas_call x1, Pallas kernels, finish(): pl.pallas_call(finish_kernel, grid=(lats // part,), out_shape=[jax.ShapeD...  4.51 us
  transfers between devices with their start and end apart: 4, of which 4 were waited for; matrix products, arithmetic and copies ran while one was open for 1% of the time, Pallas kernels for 0%

profile of v1, /device:TPU:0, one launch (start us, length us, event | category | flops | bytes accessed | tf_op | source)
XLA Modules:
  0.0 185.5 jit_solution(11631506788879902592)
XLA Ops:
  1.5 1.5 fusion.2
  5.2 1.0 copy.27.weights
  6.2 11.2 %shard_map.122 = (f32[32,274]{1,0:T(8,128)S(1)}, f32[32,274]{1,0:T(8,128)S(1)}, f32[64,274]{1,0:T(8,128)S(1)}, f32[64,274]{1,0:T(8,128)S(1)}) custom-call(f32[32,274]{1,0:T(8,128)S(1)} %get-tuple-element.91.first_lat, f32[32,274]{1,0:T(8,128)S(1)} %get-tuple-element.90.last_lat, f32[64,274]{1,0:T(8,128)S(1)} %get-tuple-element.99.first_lon, ...), custom_call_target="tpu_custom_call" | custom-call | tf_op jit(solution)/shard_map/pallas_call | solution.py:59
  17.4 1.9 %copy-done = f32[64,32,274]{2,1,0:T(8,128)S(1)} copy-done((f32[64,32,274]{2,1,0:T(8,128)S(1)}, f32[64,32,274]{2,1,0:T(8,128)}, u32[]{:S(2)}) %copy-start) | copy-done | bytes 2244632
  20.6 6.2 %shard_map.123 = (f32[512,384]{1,0:T(8,128)S(1)}, f32[512,384]{1,0:T(8,128)}) custom-call(f32[64,32,274]{2,1,0:T(8,128)S(1)} %copy-done, f32[32,274]{1,0:T(8,128)S(1)} %get-tuple-element.45.before, f32[32,274]{1,0:T(8,128)S(1)} %get-tuple-element.46.after, f32[64,274]{1,0:T(8,128)S(1)} %get-tuple-element.47.left, f32[64,274]{1,0:T(8,128)S(1)} %get-tuple-element.48.right, ...), custom_call_target="tpu_custom_call" | custom-call | tf_op jit(solution)/shard_map/pallas_call | solution.py:59
  27.7 2.1 %constant_dynamic-slice_fusion = (f32[274,1024]{1,0:T(8,128)S(1)}, f32[274,1024]{1,0:T(8,128)S(1)}) fusion(f32[548,1024]{1,0:T(8,128)} %param.14, s32[]{:T(128)S(6)} %select_n.30, s32[]{:T(128)S(6)} %select_n.29), kind=kLoop, calls=%fused_computation.9 | loop fusion | bytes 4489224 | tf_op jit(solution)/shard_map/dynamic_slice | solution.py:394
  30.4 1.2 copy-done.3
  31.6 22.4 %shard_map.124 = (f32[512,384]{1,0:T(8,128)S(1)}, f32[512,384]{1,0:T(8,128)S(1)}, f32[8,128]{1,0:T(8,128)S(1)}) custom-call(f32[512,384]{1,0:T(8,128)S(1)} %copy-done.6, f32[512,384]{1,0:T(8,128)} %collective-permute-done.other, bf16[512,1024]{1,0:T(8,128)(2,1)S(1)} %copy-done.2, bf16[512,1024]{1,0:T(8,128)(2,1)S(1)} %copy-done.3, ...), custom_call_target="tpu_custom_call" | custom-call | tf_op jit(solution)/shard_map/pallas_call | solution.py:59
  54.0 14.9 %collective-permute-start.1 = (f32[512,384]{1,0:T(8,128)S(1)}, f32[512,384]{1,0:T(8,128)S(1)}, u32[]{:S(2)}, u32[]{:S(2)}) collective-permute-start(f32[512,384]{1,0:T(8,128)S(1)} %get-tuple-element.52), channel_id=1, source_target_pairs={{0,16},{16,0},{1,17},{17,1},{2,18},{18,2},{3,19},{19,3},{4,20},{20... | collective-permute-start | bytes 2359304 | tf_op jit(solution)/shard_map/ppermute | solution.py:360
  68.9 1.9 %collective-permute-done.1.other = f32[512,384]{1,0:T(8,128)S(1)} collective-permute-done((f32[512,384]{1,0:T(8,128)S(1)}, f32[512,384]{1,0:T(8,128)S(1)}, u32[]{:S(2)}, u32[]{:S(2)}) %collective-permute-start.1) | collective-permute-done | bytes 786464 | tf_op jit(solution)/shard_map/ppermute | solution.py:360
  70.8 5.4 %shard_map.125 = (f32[2048,384]{1,0:T(8,128)S(1)}, f32[32,274]{1,0:T(8,128)S(1)}, f32[32,274]{1,0:T(8,128)S(1)}, f32[64,274]{1,0:T(8,128)S(1)}, f32[64,274]{1,0:T(8,128)S(1)}) custom-call(f32[512,384]{1,0:T(8,128)S(1)} %get-tuple-element.51.own, f32[512,384]{1,0:T(8,128)S(1)} %collective-permute-done.1.other, f32[64,32,4]{2,1,0:T(8,128)S(1)} %copy.27.weights, ...), custom_call_target="tpu_custom_call" | custom-call | tf_op jit(solution)/shard_map/pallas_call | solution.py:59
  76.2 8.9 %shard_map.126 = (f32[32,274]{1,0:T(8,128)S(1)}, f32[32,274]{1,0:T(8,128)S(1)}, f32[64,274]{1,0:T(8,128)S(1)}, f32[64,274]{1,0:T(8,128)S(1)}) custom-call(f32[32,274]{1,0:T(8,128)S(1)} %get-tuple-element.54.first_lat, f32[32,274]{1,0:T(8,128)S(1)} %get-tuple-element.55.last_lat, f32[64,274]{1,0:T(8,128)S(1)} %get-tuple-element.56.first_lon, ...), custom_call_target="tpu_custom_call" | custom-call | tf_op jit(solution)/shard_map/pallas_call | solution.py:59
  85.1 6.0 %shard_map.127 = (f32[64,32,274]{2,1,0:T(8,128)S(1)}, f32[32,274]{1,0:T(8,128)S(1)}, f32[32,274]{1,0:T(8,128)S(1)}, f32[64,274]{1,0:T(8,128)S(1)}, f32[64,274]{1,0:T(8,128)S(1)}, /*index=5*/f32[8,128]{1,0:T(8,128)S(1)}) custom-call(f32[2048,384]{1,0:T(8,128)S(1)} %get-tuple-element.53.spread, f32[32,274]{1,0:T(8,128)S(1)} %get-tuple-element.58.before, ...), custom_call_target="tpu_custom_call" | custom-call | tf_op jit(solution)/shard_map/pallas_call | solution.py:59
  91.1 9.1 %shard_map.128 = (f32[32,274]{1,0:T(8,128)S(1)}, f32[32,274]{1,0:T(8,128)S(1)}, f32[64,274]{1,0:T(8,128)S(1)}, f32[64,274]{1,0:T(8,128)S(1)}) custom-call(f32[32,274]{1,0:T(8,128)S(1)} %get-tuple-element.63.first_lat, f32[32,274]{1,0:T(8,128)S(1)} %get-tuple-element.64.last_lat, f32[64,274]{1,0:T(8,128)S(1)} %get-tuple-element.65.first_lon, ...), custom_call_target="tpu_custom_call" | custom-call | tf_op jit(solution)/shard_map/pallas_call | solution.py:59
  100.2 5.6 %shard_map.129 = (f32[512,384]{1,0:T(8,128)S(1)}, f32[512,384]{1,0:T(8,128)S(1)}) custom-call(f32[64,32,274]{2,1,0:T(8,128)S(1)} %get-tuple-element.62.field.w, f32[32,274]{1,0:T(8,128)S(1)} %get-tuple-element.67.before, f32[32,274]{1,0:T(8,128)S(1)} %get-tuple-element.68.after, f32[64,274]{1,0:T(8,128)S(1)} %get-tuple-element.69.left, ...), custom_call_target="tpu_custom_call" | custom-call | tf_op jit(solution)/shard_map/pallas_call | solution.py:59
  105.9 2.3 %collective-permute-done.2.other = f32[512,384]{1,0:T(8,128)S(1)} collective-permute-done((f32[512,384]{1,0:T(8,128)S(1)}, f32[512,384]{1,0:T(8,128)S(1)}, u32[]{:S(2)}, u32[]{:S(2)}) %collective-permute-start.2) | collective-permute-done | bytes 786464 | tf_op jit(solution)/shard_map/ppermute | solution.py:360
  108.1 22.4 %shard_map.130 = (f32[512,384]{1,0:T(8,128)S(1)}, f32[512,384]{1,0:T(8,128)S(1)}, f32[8,128]{1,0:T(8,128)}) custom-call(f32[512,384]{1,0:T(8,128)S(1)} %get-tuple-element.71.own, f32[512,384]{1,0:T(8,128)S(1)} %collective-permute-done.2.other, bf16[512,1024]{1,0:T(8,128)(2,1)S(1)} %copy-done.2, bf16[512,1024]{1,0:T(8,128)(2,1)S(1)} %copy-done.4, ...), custom_call_target="tpu_custom_call" | custom-call | tf_op jit(solution)/shard_map/pallas_call | solution.py:59
  130.5 14.8 %collective-permute-start.3 = (f32[512,384]{1,0:T(8,128)S(1)}, f32[512,384]{1,0:T(8,128)S(1)}, u32[]{:S(2)}, u32[]{:S(2)}) collective-permute-start(f32[512,384]{1,0:T(8,128)S(1)} %get-tuple-element.74), channel_id=1, source_target_pairs={{0,16},{16,0},{1,17},{17,1},{2,18},{18,2},{3,19},{19,3},{4,20},{20... | collective-permute-start | bytes 2359304 | tf_op jit(solution)/shard_map/ppermute | solution.py:360
  145.3 1.9 %collective-permute-done.3.other = f32[512,384]{1,0:T(8,128)S(1)} collective-permute-done((f32[512,384]{1,0:T(8,128)S(1)}, f32[512,384]{1,0:T(8,128)S(1)}, u32[]{:S(2)}, u32[]{:S(2)}) %collective-permute-start.3) | collective-permute-done | bytes 786464 | tf_op jit(solution)/shard_map/ppermute | solution.py:360
  147.2 5.4 %shard_map.131 = (f32[2048,384]{1,0:T(8,128)S(1)}, f32[32,274]{1,0:T(8,128)S(1)}, f32[32,274]{1,0:T(8,128)S(1)}, f32[64,274]{1,0:T(8,128)S(1)}, f32[64,274]{1,0:T(8,128)S(1)}) custom-call(f32[512,384]{1,0:T(8,128)S(1)} %get-tuple-element.73.own, f32[512,384]{1,0:T(8,128)S(1)} %collective-permute-done.3.other, f32[64,32,4]{2,1,0:T(8,128)S(1)} %copy.27.weights, ...), custom_call_target="tpu_custom_call" | custom-call | tf_op jit(solution)/shard_map/pallas_call | solution.py:59
  152.7 8.8 %shard_map.132 = (f32[32,274]{1,0:T(8,128)S(1)}, f32[32,274]{1,0:T(8,128)S(1)}, f32[64,274]{1,0:T(8,128)S(1)}, f32[64,274]{1,0:T(8,128)S(1)}) custom-call(f32[32,274]{1,0:T(8,128)S(1)} %get-tuple-element.76.first_lat, f32[32,274]{1,0:T(8,128)S(1)} %get-tuple-element.77.last_lat, f32[64,274]{1,0:T(8,128)S(1)} %get-tuple-element.78.first_lon, ...), custom_call_target="tpu_custom_call" | custom-call | tf_op jit(solution)/shard_map/pallas_call | solution.py:59
  161.5 6.3 %shard_map.133 = (f32[64,32,274]{2,1,0:T(8,128)S(1)}, f32[8,128]{1,0:T(8,128)S(1)}) custom-call(f32[2048,384]{1,0:T(8,128)S(1)} %get-tuple-element.75.spread, f32[32,274]{1,0:T(8,128)S(1)} %get-tuple-element.80.before, f32[32,274]{1,0:T(8,128)S(1)} %get-tuple-element.81.after, f32[64,274]{1,0:T(8,128)S(1)} %get-tuple-element.82.left, ...), custom_call_target="tpu_custom_call" | custom-call | tf_op jit(solution)/shard_map/pallas_call | solution.py:59
  167.8 13.2 %shard_map.134.sums = f32[8,128]{1,0:T(8,128)S(1)} custom-call(f32[8,128]{1,0:T(8,128)S(1)} %get-tuple-element.85.x_ref), custom_call_target="tpu_custom_call" | custom-call | tf_op jit(solution)/shard_map/pallas_call | solution.py:59
  181.0 4.5 %shard_map.135 = (f32[64,32,274]{2,1,0:T(8,128)}, f32[64,32,274]{2,1,0:T(8,128)}) custom-call(f32[8,128]{1,0:T(8,128)S(1)} %shard_map.134.sums, f32[8,128]{1,0:T(8,128)S(1)} %get-tuple-element.86.scale, f32[64,32,274]{2,1,0:T(8,128)S(1)} %copy-done.1, f32[64,32,274]{2,1,0:T(8,128)S(1)} %get-tuple-element.62.field.w, f32[64,32,274]{2,1,0:T(8,128)S(1)} %get-tuple-element.87.x), custom_call_target="tpu_custom_call" | custom-call | tf_op jit(solution)/shard_map/pallas_call | solution.py:349
  (31 shorter events, 5.9 us)
Async XLA Ops:
  17.4 1.9 %copy-start = (f32[64,32,274]{2,1,0:T(8,128)S(1)}, f32[64,32,274]{2,1,0:T(8,128)}, u32[]{:S(2)}) copy-start(f32[64,32,274]{2,1,0:T(8,128)} %b.1) | copy-start | bytes 6733828
  19.3 0.7 copy-start.7
  20.0 0.7 copy-start.9
  26.8 0.9 copy-start.5
  27.7 2.6 %copy-start.2 = (bf16[512,1024]{1,0:T(8,128)(2,1)S(1)}, bf16[512,1024]{1,0:T(8,128)(2,1)}, u32[]{:S(2)}) copy-start(bf16[512,1024]{1,0:T(8,128)(2,1)} %gate_one.3) | copy-start | bytes 3145732
  27.7 2.6 %copy-start.10 = (s32[32]{0:T(128)S(1)}, s32[32]{0:T(128)}, u32[]{:S(2)}) copy-start(s32[32]{0:T(128)} %counts.11) | copy-start | bytes 388
  27.7 2.6 %collective-permute-start = (f32[512,384]{1,0:T(8,128)}, f32[512,384]{1,0:T(8,128)}, u32[]{:S(2)}, u32[]{:S(2)}) collective-permute-start(f32[512,384]{1,0:T(8,128)} %get-tuple-element.50), channel_id=1, source_target_pairs={{0,16},{16,0},{1,17},{17,1},{2,18},{18,2},{3,19},{19,3},{4,20},{20... | collective-permute-start | bytes 2359304 | tf_op jit(solution)/shard_map/ppermute | solution.py:360
  27.7 2.6 %copy-start.6 = (f32[512,384]{1,0:T(8,128)S(1)}, f32[512,384]{1,0:T(8,128)}, u32[]{:S(2)}) copy-start(f32[512,384]{1,0:T(8,128)} %copy-done.5) | copy-start | bytes 2359300
  30.3 1.2 copy-start.3
  31.6 39.2 %copy-start.8 = (s32[2,512]{1,0:T(2,128)S(1)}, s32[2,512]{1,0:T(2,128)}, u32[]{:S(2)}) copy-start(s32[2,512]{1,0:T(2,128)} %cells.7) | copy-start | bytes 12292
  31.6 53.5 %copy-start.1 = (f32[64,32,274]{2,1,0:T(8,128)S(1)}, f32[64,32,274]{2,1,0:T(8,128)}, u32[]{:S(2)}) copy-start(f32[64,32,274]{2,1,0:T(8,128)} %b.1) | copy-start | bytes 6733828
  54.0 16.8 %collective-permute-start.1 = (f32[512,384]{1,0:T(8,128)S(1)}, f32[512,384]{1,0:T(8,128)S(1)}, u32[]{:S(2)}, u32[]{:S(2)}) collective-permute-start(f32[512,384]{1,0:T(8,128)S(1)} %get-tuple-element.52), channel_id=1, source_target_pairs={{0,16},{16,0},{1,17},{17,1},{2,18},{18,2},{3,19},{19,3},{4,20},{20... | collective-permute-start | bytes 2359304 | tf_op jit(solution)/shard_map/ppermute | solution.py:360
  91.1 17.0 %copy-start.4 = (bf16[512,1024]{1,0:T(8,128)(2,1)S(1)}, bf16[512,1024]{1,0:T(8,128)(2,1)}, u32[]{:S(2)}) copy-start(bf16[512,1024]{1,0:T(8,128)(2,1)} %gate_two.3) | copy-start | bytes 3145732
  105.8 2.4 %collective-permute-start.2 = (f32[512,384]{1,0:T(8,128)S(1)}, f32[512,384]{1,0:T(8,128)S(1)}, u32[]{:S(2)}, u32[]{:S(2)}) collective-permute-start(f32[512,384]{1,0:T(8,128)S(1)} %get-tuple-element.72), channel_id=1, source_target_pairs={{0,16},{16,0},{1,17},{17,1},{2,18},{18,2},{3,19},{19,3},{4,20},{20... | collective-permute-start | bytes 2359304 | tf_op jit(solution)/shard_map/ppermute | solution.py:360
  130.5 16.7 %collective-permute-start.3 = (f32[512,384]{1,0:T(8,128)S(1)}, f32[512,384]{1,0:T(8,128)S(1)}, u32[]{:S(2)}, u32[]{:S(2)}) collective-permute-start(f32[512,384]{1,0:T(8,128)S(1)} %get-tuple-element.74), channel_id=1, source_target_pairs={{0,16},{16,0},{1,17},{17,1},{2,18},{18,2},{3,19},{19,3},{4,20},{20... | collective-permute-start | bytes 2359304 | tf_op jit(solution)/shard_map/ppermute | solution.py:360

commit v2 on v1

--- a/solution.py
+++ b/solution.py
@@ -54,7 +54,7 @@
 
 
 def call(kernel, grant, shapes, specs, scratch, *operands, **params):
-    out = [jax.ShapeDtypeStruct(shape, jnp.float32) for shape in shapes]
+    out = [jax.ShapeDtypeStruct(shape[:2] if shape[-1] == "half" else shape, jnp.bfloat16 if shape[-1] == "half" else jnp.float32) for shape in shapes]
     params = pltpu.CompilerParams(vmem_limit_bytes=grant * MIB, **params)
     return pl.pallas_call(
         kernel,
@@ -256,37 +256,48 @@
     rest[-1][...] = block
 
 
-def network_kernel(own, other, gate_one, gate_two, w_own, w_other, w_mid, w_out, cov, counts, d_own, d_other, scale_out, *scratch):
-    pairs = [scratch[2 * k : 2 * k + 2] for k in range(5)]
-    squares = []
-    for full, (high, low) in zip((w_own, w_other, w_mid, w_out, cov), pairs):
-        chunk = 32
+def split_kernel(wide, w_own, w_other, w_mid, w_out, cov, *outs):
+    pairs = [outs[2 * k : 2 * k + 2] for k in range(4)]
+    scale_out = outs[8]
+    for pair in (pairs[0], pairs[2], pairs[3]):
+        for half in pair:
+            half[...] = jnp.zeros_like(half)
+    chunk = 32
+
+    def squares(full, pair, base):
+        high, low = pair
         rows, columns = full.shape
 
-        def store(start, value, high=high, low=low, columns=columns):
+        def store(start, value):
             lines = pl.ds(start, chunk)
             rounded = value.astype(jnp.bfloat16)
             high[lines, :columns] = rounded
             low[lines, :columns] = (value - rounded.astype(jnp.float32)).astype(jnp.bfloat16)
-            return value * value
-
-        def split(c, total, full=full, store=store):
+            square = value * value
+            return (square[:8] + square[8:16]) + (square[16:24] + square[24:])
+
+        def split(c, total):
             start = pl.multiple_of(c * chunk, chunk)
-            return total + store(start, full[pl.ds(start, chunk)])
-
-        if high.shape != full.shape:
-            high[...] = jnp.zeros_like(high)
-            low[...] = jnp.zeros_like(low)
-        total = lax.fori_loop(0, rows // chunk, split, jnp.zeros((chunk, columns), jnp.float32))
+            return total + store(pl.multiple_of(base + start, chunk), full[pl.ds(start, chunk)])
+
+        total = lax.fori_loop(0, rows // chunk, split, jnp.zeros((8, columns), jnp.float32))
         left = rows % chunk
         if left:
             rest = jnp.concatenate([full[rows - left :], jnp.zeros((chunk - left, columns), jnp.float32)], axis=0)
-            total = total + store(rows - left, rest)
-        squares.append(jnp.sum(total, axis=(0, 1), keepdims=True))
-    bound = (squares[0] + squares[1]) * squares[2] * squares[3] * jnp.sqrt(squares[4])
-    scale = 1.0 / jnp.maximum(bound, 1.0)
+            total = total + store(base + rows - left, rest)
+        return jnp.sum(total, axis=(0, 1), keepdims=True)
+
+    first = squares(w_own, pairs[0], 0) + squares(w_other, pairs[0], wide)
+    bound = first * squares(w_mid, pairs[1], 0) * squares(w_out, pairs[2], 0)
+    scale = 1.0 / jnp.maximum(bound * jnp.sqrt(squares(cov, pairs[3], 0)), 1.0)
     scale_out[...] = jnp.broadcast_to(scale, scale_out.shape)
-    p_own, p_other, p_mid, p_out, p_cov = pairs
+
+
+def network_kernel(own, other, gate_one, gate_two, *rest):
+    p_in, p_mid, p_out, p_cov = (rest[2 * k : 2 * k + 2] for k in range(4))
+    scale, counts, d_own, d_other = rest[8:]
+    factor = scale[0:1, 0:1]
+    wide = own.shape[1]
 
     def product(value, pair, back=False):
         dims = (((1,), (1 if back else 0,)), ((), ()))
@@ -304,14 +315,15 @@
     @pl.loop(0, (live + rows - 1) // rows)
     def _(j):
         lines = pl.ds(pl.multiple_of(j * rows, rows), rows)
-        g1 = gate_one[lines].astype(jnp.float32)
-        hidden = (product(own[lines], p_own) + product(other[lines], p_other)) * g1
+        columns = jnp.concatenate([own[lines], other[lines]], axis=1)
+        hidden = product(columns, p_in) * gate_one[lines].astype(jnp.float32)
         hidden = product(hidden, p_mid) * gate_two[lines].astype(jnp.float32)
-        weighted = product(product(hidden, p_out, True), p_cov) * scale
+        weighted = product(product(hidden, p_out, True), p_cov) * factor
         back = product(weighted, p_out) * gate_two[lines].astype(jnp.float32)
         back = product(back, p_mid, True) * gate_one[lines].astype(jnp.float32)
-        d_own[lines] = product(back, p_own, True)
-        d_other[lines] = product(back, p_other, True)
+        terms = product(back, p_in, True)
+        d_own[lines] = terms[:, :wide]
+        d_other[lines] = terms[:, wide:]
 
 
 def combination(scale, bb, bw, ww, wx):
@@ -393,9 +405,11 @@
     rates = channel_rates.reshape(1, width)
     halves = [lax.dynamic_slice_in_dim(weight_in, part * width, width, 0) for part in (side, 1 - side)]
     hidden = weight_in.shape[1]
-    matrices = [*halves, weight_mid, weight_out.T, inverse_cov]
-    shapes = [(wide, hidden), (wide, hidden), (hidden, hidden), (channels, hidden), (channels, channels)]
-    split_scratch = [pltpu.VMEM(shape, jnp.bfloat16) for shape in shapes for _ in range(2)]
+    hidden = weight_in.shape[1]
+    matrices = (*halves, weight_mid, weight_out.T, inverse_cov)
+    shapes = [(2 * wide, hidden), (hidden, hidden), (channels, hidden), (channels, channels)]
+    shapes = [(*shape, "half") for shape in shapes for _ in range(2)] + [(8, LANES)]
+    *pairs, scale = call(functools.partial(split_kernel, wide), 28, shapes, [VMEM] * 5, [], *matrices)
     lat_edge, lon_edge = (lons, width), (lats, width)
 
     def spread(field, edges, known, sums, is_first):
@@ -405,9 +419,8 @@
         operands = (field, *around, weights, rates, profile_cells, profile_counts)
         own, other = call(gather_kernel, 16, [(slots, wide)] * 2, specs, image, *operands)
         other = swapped(other)
-        operands = (own, other, gate_first, gate_second, *matrices, profile_counts)
-        shapes = [(slots, wide)] * 2 + [(8, LANES)]
-        own, other, scale = call(network_kernel, 46, shapes, [VMEM] * 9 + [SMEM], split_scratch, *operands)
+        operands = (own, other, gate_first, gate_second, *pairs, scale, profile_counts)
+        own, other = call(network_kernel, 36, [(slots, wide)] * 2, [VMEM] * 13 + [SMEM], [], *operands)
         other = swapped(other)
         parts = [pltpu.VMEM((lats * lons, wide), jnp.float32)] * 4
         shapes = [(lats * lons, wide), lat_edge, lat_edge, lon_edge, lon_edge]
@@ -417,11 +430,11 @@
         shapes = [field.shape] + ([lat_edge, lat_edge, lon_edge, lon_edge] if is_first else []) + [(8, LANES)]
         operands = (summed, *around, weights, rates, known, sums)
         out, *edges, sums = call(functools.partial(adjoint_kernel, is_first), 16, shapes, [VMEM] * 9, [], *operands)
-        return out, edges, sums, scale
+        return out, edges, sums
 
     edges = (right_side[0], right_side[lats - 1], right_side[:, 0], right_side[:, lons - 1])
-    first, edges, sums, scale = spread(right_side, edges, right_side, jnp.zeros((8, LANES), jnp.float32), True)
-    second, _, sums, _ = spread(first, edges, first, sums, False)
+    first, edges, sums = spread(right_side, edges, right_side, jnp.zeros((8, LANES), jnp.float32), True)
+    second, _, sums = spread(first, edges, first, sums, False)
     return tuple(finish(all_sums(sums), scale, right_side, first, second))
 
 

time: 186 us -> 170 us (0.914); the launches traced: 186 us -> 172 us
  starting transfers between devices: 29.8 us -> 0.85 us
  Pallas kernels: 135 us -> 151 us
    ppermute x4, starting transfers between devices: 29.8 us -> 0.85 us  [swapped(): return lax.ppermute(value, 'side', [(0, 1), (1, 0)])]
    pallas_call x13 -> x14, Pallas kernels: 131 us -> 146 us  [call(): pl.pallas_call(kernel, out_shape=out, in_specs=specs, out_specs=[VMEM] *...]
    unnamed x22 -> x28, local copies, waits for them, and re-layouts: 5.35 us -> 7.83 us
  transfers between devices with their start and end apart: 4 -> 4, of which waited for: 4 -> 3; matrix products, arithmetic and copies ran while one was open for 1% -> 0% of each run, Pallas kernels for 0% -> 2%
where the time goes in v2:
time: 170 us; the launch traced here: 172 us
  Pallas kernels  151 us (89%)
  local copies, waits for them, and re-layouts  12.9 us (8%)
  waiting for transfers between devices  6.33 us (4%)
    pallas_call x14, Pallas kernels, call(): pl.pallas_call(kernel, out_shape=out, in_specs=specs, out_specs=[VMEM] *...  146 us
    unnamed x28, local copies, waits for them, and re-layouts  7.83 us
    ppermute x4, waiting for transfers between devices, swapped(): return lax.ppermute(value, 'side', [(0, 1), (1, 0)])  6.33 us
    pallas_call x1, Pallas kernels, finish(): pl.pallas_call(finish_kernel, grid=(lats // part,), out_shape=[jax.ShapeD...  4.48 us
  transfers between devices with their start and end apart: 4, of which 3 were waited for; matrix products, arithmetic and copies ran while one was open for 0% of the time, Pallas kernels for 2%

profile of v2, /device:TPU:0, one launch (start us, length us, event | category | flops | bytes accessed | tf_op | source)
XLA Modules:
  0.0 172.3 jit_solution(3451539096542379000)
XLA Ops:
  1.5 1.5 fusion.2
  5.2 1.0 copy.27.weights
  6.2 11.2 %shard_map.122 = (f32[32,274]{1,0:T(8,128)S(1)}, f32[32,274]{1,0:T(8,128)S(1)}, f32[64,274]{1,0:T(8,128)S(1)}, f32[64,274]{1,0:T(8,128)S(1)}) custom-call(f32[32,274]{1,0:T(8,128)S(1)} %get-tuple-element.107.first_lat, f32[32,274]{1,0:T(8,128)S(1)} %get-tuple-element.106.last_lat, f32[64,274]{1,0:T(8,128)S(1)} %get-tuple-element.115.first_lon, ...), custom_call_target="tpu_custom_call" | custom-call | tf_op jit(solution)/shard_map/pallas_call | solution.py:59
  17.4 1.9 %copy-done = f32[64,32,274]{2,1,0:T(8,128)S(1)} copy-done((f32[64,32,274]{2,1,0:T(8,128)S(1)}, f32[64,32,274]{2,1,0:T(8,128)}, u32[]{:S(2)}) %copy-start) | copy-done | bytes 2244632
  19.3 5.3 %shard_map.123 = (f32[512,384]{1,0:T(8,128)S(1)}, f32[512,384]{1,0:T(8,128)}) custom-call(f32[64,32,274]{2,1,0:T(8,128)S(1)} %copy-done, f32[32,274]{1,0:T(8,128)S(1)} %get-tuple-element.53.before, f32[32,274]{1,0:T(8,128)S(1)} %get-tuple-element.54.after, f32[64,274]{1,0:T(8,128)S(1)} %get-tuple-element.55.left, f32[64,274]{1,0:T(8,128)S(1)} %get-tuple-element.56.right, ...), custom_call_target="tpu_custom_call" | custom-call | tf_op jit(solution)/shard_map/pallas_call | solution.py:59
  25.8 1.9 %copy-done.2 = f32[1024,1024]{1,0:T(8,128)S(1)} copy-done((f32[1024,1024]{1,0:T(8,128)S(1)}, f32[1024,1024]{1,0:T(8,128)}, u32[]{:S(2)}) %copy-start.2) | copy-done | bytes 4194328
  27.7 1.7 copy-done.7
  29.4 1.4 copy-done.8
  30.8 3.6 %shard_map.124 = (bf16[768,1024]{1,0:T(8,128)(2,1)S(1)}, bf16[768,1024]{1,0:T(8,128)(2,1)S(1)}, bf16[1024,1024]{1,0:T(8,128)(2,1)S(1)}, bf16[1024,1024]{1,0:T(8,...) custom-call(f32[274,1024]{1,0:T(8,128)S(1)} %get-tuple-element.109.w, ...), custom_call_target="tpu_custom_call" | custom-call | tf_op jit(solution)/shard_map/pallas_call | solution.py:59
  34.5 14.8 %shard_map.125 = (f32[512,384]{1,0:T(8,128)S(1)}, f32[512,384]{1,0:T(8,128)S(1)}) custom-call(f32[512,384]{1,0:T(8,128)S(1)} %copy-done.10, f32[512,384]{1,0:T(8,128)} %collective-permute-done.other, bf16[512,1024]{1,0:T(8,128)(2,1)S(1)} %copy-done.3, bf16[512,1024]{1,0:T(8,128)(2,1)S(1)} %copy-done.5, bf16[768,1024]{1,0:T(8,128)(2,1)S(1)} %get-tuple-element.59.rest_0_, ...), custom_call_target="tpu_custom_call" | custom-call | tf_op jit(solution)/shard_map/pallas_call | solution.py:59
  49.8 1.9 %collective-permute-done.1.other = f32[512,384]{1,0:T(8,128)S(1)} collective-permute-done((f32[512,384]{1,0:T(8,128)S(1)}, f32[512,384]{1,0:T(8,128)S(1)}, u32[]{:S(2)}, u32[]{:S(2)}) %collective-permute-start.1) | collective-permute-done | bytes 786464 | tf_op jit(solution)/shard_map/ppermute | solution.py:372
  51.7 3.8 %shard_map.126 = (f32[2048,384]{1,0:T(8,128)S(1)}, f32[32,274]{1,0:T(8,128)S(1)}, f32[32,274]{1,0:T(8,128)S(1)}, f32[64,274]{1,0:T(8,128)S(1)}, f32[64,274]{1,0:T(8,128)S(1)}) custom-call(f32[512,384]{1,0:T(8,128)S(1)} %get-tuple-element.68.own, f32[512,384]{1,0:T(8,128)S(1)} %collective-permute-done.1.other, f32[64,32,4]{2,1,0:T(8,128)S(1)} %copy.27.weights, ...), custom_call_target="tpu_custom_call" | custom-call | tf_op jit(solution)/shard_map/pallas_call | solution.py:59
  55.6 24.3 %shard_map.127 = (f32[32,274]{1,0:T(8,128)S(1)}, f32[32,274]{1,0:T(8,128)S(1)}, f32[64,274]{1,0:T(8,128)S(1)}, f32[64,274]{1,0:T(8,128)S(1)}) custom-call(f32[32,274]{1,0:T(8,128)S(1)} %get-tuple-element.71.first_lat, f32[32,274]{1,0:T(8,128)S(1)} %get-tuple-element.72.last_lat, f32[64,274]{1,0:T(8,128)S(1)} %get-tuple-element.73.first_lon, ...), custom_call_target="tpu_custom_call" | custom-call | tf_op jit(solution)/shard_map/pallas_call | solution.py:59
  79.9 6.0 %shard_map.128 = (f32[64,32,274]{2,1,0:T(8,128)S(1)}, f32[32,274]{1,0:T(8,128)S(1)}, f32[32,274]{1,0:T(8,128)S(1)}, f32[64,274]{1,0:T(8,128)S(1)}, f32[64,274]{1,0:T(8,128)S(1)}, /*index=5*/f32[8,128]{1,0:T(8,128)S(1)}) custom-call(f32[2048,384]{1,0:T(8,128)S(1)} %get-tuple-element.70.spread, f32[32,274]{1,0:T(8,128)S(1)} %get-tuple-element.75.before, ...), custom_call_target="tpu_custom_call" | custom-call | tf_op jit(solution)/shard_map/pallas_call | solution.py:59
  85.9 8.3 %shard_map.129 = (f32[32,274]{1,0:T(8,128)S(1)}, f32[32,274]{1,0:T(8,128)S(1)}, f32[64,274]{1,0:T(8,128)S(1)}, f32[64,274]{1,0:T(8,128)S(1)}) custom-call(f32[32,274]{1,0:T(8,128)S(1)} %get-tuple-element.80.first_lat, f32[32,274]{1,0:T(8,128)S(1)} %get-tuple-element.81.last_lat, f32[64,274]{1,0:T(8,128)S(1)} %get-tuple-element.82.first_lon, ...), custom_call_target="tpu_custom_call" | custom-call | tf_op jit(solution)/shard_map/pallas_call | solution.py:59
  94.3 4.3 %shard_map.130 = (f32[512,384]{1,0:T(8,128)S(1)}, f32[512,384]{1,0:T(8,128)S(1)}) custom-call(f32[64,32,274]{2,1,0:T(8,128)S(1)} %get-tuple-element.79.field.w, f32[32,274]{1,0:T(8,128)S(1)} %get-tuple-element.84.before, f32[32,274]{1,0:T(8,128)S(1)} %get-tuple-element.85.after, f32[64,274]{1,0:T(8,128)S(1)} %get-tuple-element.86.left, ...), custom_call_target="tpu_custom_call" | custom-call | tf_op jit(solution)/shard_map/pallas_call | solution.py:59
  98.7 2.3 %collective-permute-done.2.other = f32[512,384]{1,0:T(8,128)S(1)} collective-permute-done((f32[512,384]{1,0:T(8,128)S(1)}, f32[512,384]{1,0:T(8,128)S(1)}, u32[]{:S(2)}, u32[]{:S(2)}) %collective-permute-start.2) | collective-permute-done | bytes 786464 | tf_op jit(solution)/shard_map/ppermute | solution.py:372
  100.9 13.9 %shard_map.131 = (f32[512,384]{1,0:T(8,128)S(1)}, f32[512,384]{1,0:T(8,128)S(1)}) custom-call(f32[512,384]{1,0:T(8,128)S(1)} %get-tuple-element.88.own, f32[512,384]{1,0:T(8,128)S(1)} %collective-permute-done.2.other, bf16[512,1024]{1,0:T(8,128)(2,1)S(1)} %copy-done.4, bf16[512,1024]{1,0:T(8,128)(2,1)S(1)} %copy-done.6, ...), custom_call_target="tpu_custom_call" | custom-call | tf_op jit(solution)/shard_map/pallas_call | solution.py:59
  115.0 2.1 %collective-permute-done.3.other = f32[512,384]{1,0:T(8,128)S(1)} collective-permute-done((f32[512,384]{1,0:T(8,128)S(1)}, f32[512,384]{1,0:T(8,128)S(1)}, u32[]{:S(2)}, u32[]{:S(2)}) %collective-permute-start.3) | collective-permute-done | bytes 786464 | tf_op jit(solution)/shard_map/ppermute | solution.py:372
  117.2 3.8 %shard_map.132 = (f32[2048,384]{1,0:T(8,128)S(1)}, f32[32,274]{1,0:T(8,128)S(1)}, f32[32,274]{1,0:T(8,128)S(1)}, f32[64,274]{1,0:T(8,128)S(1)}, f32[64,274]{1,0:T(8,128)S(1)}) custom-call(f32[512,384]{1,0:T(8,128)S(1)} %get-tuple-element.90.own, f32[512,384]{1,0:T(8,128)S(1)} %collective-permute-done.3.other, f32[64,32,4]{2,1,0:T(8,128)S(1)} %copy.27.weights, ...), custom_call_target="tpu_custom_call" | custom-call | tf_op jit(solution)/shard_map/pallas_call | solution.py:59
  121.0 25.6 %shard_map.133 = (f32[32,274]{1,0:T(8,128)S(1)}, f32[32,274]{1,0:T(8,128)S(1)}, f32[64,274]{1,0:T(8,128)S(1)}, f32[64,274]{1,0:T(8,128)S(1)}) custom-call(f32[32,274]{1,0:T(8,128)S(1)} %get-tuple-element.93.first_lat, f32[32,274]{1,0:T(8,128)S(1)} %get-tuple-element.94.last_lat, f32[64,274]{1,0:T(8,128)S(1)} %get-tuple-element.95.first_lon, ...), custom_call_target="tpu_custom_call" | custom-call | tf_op jit(solution)/shard_map/pallas_call | solution.py:59
  146.6 6.2 %shard_map.134 = (f32[64,32,274]{2,1,0:T(8,128)S(1)}, f32[8,128]{1,0:T(8,128)S(1)}) custom-call(f32[2048,384]{1,0:T(8,128)S(1)} %get-tuple-element.92.spread, f32[32,274]{1,0:T(8,128)S(1)} %get-tuple-element.97.before, f32[32,274]{1,0:T(8,128)S(1)} %get-tuple-element.98.after, f32[64,274]{1,0:T(8,128)S(1)} %get-tuple-element.99.left, ...), custom_call_target="tpu_custom_call" | custom-call | tf_op jit(solution)/shard_map/pallas_call | solution.py:59
  152.9 14.9 %shard_map.135.sums = f32[8,128]{1,0:T(8,128)S(1)} custom-call(f32[8,128]{1,0:T(8,128)S(1)} %get-tuple-element.102.x_ref), custom_call_target="tpu_custom_call" | custom-call | tf_op jit(solution)/shard_map/pallas_call | solution.py:59
  167.8 4.5 %shard_map.136 = (f32[64,32,274]{2,1,0:T(8,128)}, f32[64,32,274]{2,1,0:T(8,128)}) custom-call(f32[8,128]{1,0:T(8,128)S(1)} %shard_map.135.sums, f32[8,128]{1,0:T(8,128)S(1)} %get-tuple-element.67.rest_8_.scale, f32[64,32,274]{2,1,0:T(8,128)S(1)} %copy-done.1, f32[64,32,274]{2,1,0:T(8,128)S(1)} %get-tuple-element.79.field.w, ...), custom_call_target="tpu_custom_call" | custom-call | tf_op jit(solution)/shard_map/pallas_call | solution.py:361
  (38 shorter events, 5.1 us)
Async XLA Ops:
  0.6 16.8 %copy-start.12 = (s32[32]{0:T(128)S(1)}, s32[32]{0:T(128)}, u32[]{:S(2)}) copy-start(s32[32]{0:T(128)} %counts.7) | copy-start | bytes 388
  0.6 16.8 %copy-start.11 = (s32[2,512]{1,0:T(2,128)S(1)}, s32[2,512]{1,0:T(2,128)}, u32[]{:S(2)}) copy-start(s32[2,512]{1,0:T(2,128)} %cells.7) | copy-start | bytes 12292
  17.4 1.9 %copy-start = (f32[64,32,274]{2,1,0:T(8,128)S(1)}, f32[64,32,274]{2,1,0:T(8,128)}, u32[]{:S(2)}) copy-start(f32[64,32,274]{2,1,0:T(8,128)} %b.1) | copy-start | bytes 6733828
  19.3 6.2 %copy-start.13 = (f32[548,1024]{1,0:T(8,128)S(1)}, f32[548,1024]{1,0:T(8,128)}, u32[]{:S(2)}) copy-start(f32[548,1024]{1,0:T(8,128)} %param.14) | copy-start | bytes 6733828
  24.6 0.9 copy-start.9
  25.5 8.9 %collective-permute-start = (f32[512,384]{1,0:T(8,128)}, f32[512,384]{1,0:T(8,128)}, u32[]{:S(2)}, u32[]{:S(2)}) collective-permute-start(f32[512,384]{1,0:T(8,128)} %get-tuple-element.58), channel_id=1, source_target_pairs={{0,16},{16,0},{1,17},{17,1},{2,18},{18,2},{3,19},{19,3},{4,20},{20... | collective-permute-start | bytes 2359304 | tf_op jit(solution)/shard_map/ppermute | solution.py:372
  25.5 2.2 %copy-start.2 = (f32[1024,1024]{1,0:T(8,128)S(1)}, f32[1024,1024]{1,0:T(8,128)}, u32[]{:S(2)}) copy-start(f32[1024,1024]{1,0:T(8,128)} %w_mid.1) | copy-start | bytes 12582916
  27.7 1.7 copy-start.7
  29.4 1.4 copy-start.8
  30.8 3.6 %copy-start.3 = (bf16[512,1024]{1,0:T(8,128)(2,1)S(1)}, bf16[512,1024]{1,0:T(8,128)(2,1)}, u32[]{:S(2)}) copy-start(bf16[512,1024]{1,0:T(8,128)(2,1)} %gate_one.3) | copy-start | bytes 3145732
  30.8 3.6 %copy-start.5 = (bf16[512,1024]{1,0:T(8,128)(2,1)S(1)}, bf16[512,1024]{1,0:T(8,128)(2,1)}, u32[]{:S(2)}) copy-start(bf16[512,1024]{1,0:T(8,128)(2,1)} %gate_two.3) | copy-start | bytes 3145732
  30.8 3.6 %copy-start.10 = (f32[512,384]{1,0:T(8,128)S(1)}, f32[512,384]{1,0:T(8,128)}, u32[]{:S(2)}) copy-start(f32[512,384]{1,0:T(8,128)} %copy-done.9) | copy-start | bytes 2359300
  34.5 45.5 %copy-start.1 = (f32[64,32,274]{2,1,0:T(8,128)S(1)}, f32[64,32,274]{2,1,0:T(8,128)}, u32[]{:S(2)}) copy-start(f32[64,32,274]{2,1,0:T(8,128)} %b.1) | copy-start | bytes 6733828
  49.3 2.5 %collective-permute-start.1 = (f32[512,384]{1,0:T(8,128)S(1)}, f32[512,384]{1,0:T(8,128)S(1)}, u32[]{:S(2)}, u32[]{:S(2)}) collective-permute-start(f32[512,384]{1,0:T(8,128)S(1)} %get-tuple-element.69), channel_id=1, source_target_pairs={{0,16},{16,0},{1,17},{17,1},{2,18},{18,2},{3,19},{19,3},{4,20},{20... | collective-permute-start | bytes 2359304 | tf_op jit(solution)/shard_map/ppermute | solution.py:372
  94.2 6.7 %copy-start.4 = (bf16[512,1024]{1,0:T(8,128)(2,1)S(1)}, bf16[512,1024]{1,0:T(8,128)(2,1)}, u32[]{:S(2)}) copy-start(bf16[512,1024]{1,0:T(8,128)(2,1)} %gate_one.3) | copy-start | bytes 3145732
  94.3 6.7 %copy-start.6 = (bf16[512,1024]{1,0:T(8,128)(2,1)S(1)}, bf16[512,1024]{1,0:T(8,128)(2,1)}, u32[]{:S(2)}) copy-start(bf16[512,1024]{1,0:T(8,128)(2,1)} %gate_two.3) | copy-start | bytes 3145732
  98.6 2.4 %collective-permute-start.2 = (f32[512,384]{1,0:T(8,128)S(1)}, f32[512,384]{1,0:T(8,128)S(1)}, u32[]{:S(2)}, u32[]{:S(2)}) collective-permute-start(f32[512,384]{1,0:T(8,128)S(1)} %get-tuple-element.89), channel_id=1, source_target_pairs={{0,16},{16,0},{1,17},{17,1},{2,18},{18,2},{3,19},{19,3},{4,20},{20... | collective-permute-start | bytes 2359304 | tf_op jit(solution)/shard_map/ppermute | solution.py:372
  114.8 2.4 %collective-permute-start.3 = (f32[512,384]{1,0:T(8,128)S(1)}, f32[512,384]{1,0:T(8,128)S(1)}, u32[]{:S(2)}, u32[]{:S(2)}) collective-permute-start(f32[512,384]{1,0:T(8,128)S(1)} %get-tuple-element.91), channel_id=1, source_target_pairs={{0,16},{16,0},{1,17},{17,1},{2,18},{18,2},{3,19},{19,3},{4,20},{20... | collective-permute-start | bytes 2359304 | tf_op jit(solution)/shard_map/ppermute | solution.py:372

commit v3 on v2

--- a/solution.py
+++ b/solution.py
@@ -307,7 +307,9 @@
         def dot(left, right):
             return lax.dot_general(left, right[...], dims, preferred_element_type=jnp.float32)
 
-        return dot(high, pair[0]) + (dot(low, pair[0]) + dot(high, pair[1]))
+        count = value.shape[0]
+        both = dot(jnp.concatenate([high, low], axis=0), pair[0])
+        return both[:count] + (both[count:] + dot(high, pair[1]))
 
     rows = min(256, own.shape[0])
     live = live_counts(counts)[0][1]

time: 170 us -> 157 us (0.924); the launches traced: 172 us -> 157 us
  Pallas kernels: 151 us -> 136 us
    pallas_call x14, Pallas kernels: 146 us -> 131 us  [call(): pl.pallas_call(kernel, out_shape=out, in_specs=specs, out_specs=[VMEM] *...]
where the time goes in v3:
time: 157 us
  Pallas kernels  136 us (87%)
  local copies, waits for them, and re-layouts  12.9 us (8%)
  waiting for transfers between devices  6.35 us (4%)
    pallas_call x14, Pallas kernels, call(): pl.pallas_call(kernel, out_shape=out, in_specs=specs, out_specs=[VMEM] *...  131 us
    unnamed x28, local copies, waits for them, and re-layouts  7.83 us
    ppermute x4, waiting for transfers between devices, swapped(): return lax.ppermute(value, 'side', [(0, 1), (1, 0)])  6.35 us
    pallas_call x1, Pallas kernels, finish(): pl.pallas_call(finish_kernel, grid=(lats // part,), out_shape=[jax.ShapeD...  4.48 us
  transfers between devices with their start and end apart: 4, of which 3 were waited for; matrix products, arithmetic and copies ran while one was open for 0% of the time, Pallas kernels for 2%

profile of v3, /device:TPU:0, one launch (start us, length us, event | category | flops | bytes accessed | tf_op | source)
XLA Modules:
  0.0 157.3 jit_solution(12521781857846587268)
XLA Ops:
  1.5 1.5 fusion.2
  5.2 1.0 copy.27.weights
  6.2 11.2 %shard_map.122 = (f32[32,274]{1,0:T(8,128)S(1)}, f32[32,274]{1,0:T(8,128)S(1)}, f32[64,274]{1,0:T(8,128)S(1)}, f32[64,274]{1,0:T(8,128)S(1)}) custom-call(f32[32,274]{1,0:T(8,128)S(1)} %get-tuple-element.107.first_lat, f32[32,274]{1,0:T(8,128)S(1)} %get-tuple-element.106.last_lat, f32[64,274]{1,0:T(8,128)S(1)} %get-tuple-element.115.first_lon, ...), custom_call_target="tpu_custom_call" | custom-call | tf_op jit(solution)/shard_map/pallas_call | solution.py:59
  17.4 1.9 %copy-done = f32[64,32,274]{2,1,0:T(8,128)S(1)} copy-done((f32[64,32,274]{2,1,0:T(8,128)S(1)}, f32[64,32,274]{2,1,0:T(8,128)}, u32[]{:S(2)}) %copy-start) | copy-done | bytes 2244632
  19.3 5.2 %shard_map.123 = (f32[512,384]{1,0:T(8,128)S(1)}, f32[512,384]{1,0:T(8,128)}) custom-call(f32[64,32,274]{2,1,0:T(8,128)S(1)} %copy-done, f32[32,274]{1,0:T(8,128)S(1)} %get-tuple-element.53.before, f32[32,274]{1,0:T(8,128)S(1)} %get-tuple-element.54.after, f32[64,274]{1,0:T(8,128)S(1)} %get-tuple-element.55.left, f32[64,274]{1,0:T(8,128)S(1)} %get-tuple-element.56.right, ...), custom_call_target="tpu_custom_call" | custom-call | tf_op jit(solution)/shard_map/pallas_call | solution.py:59
  25.7 1.9 %copy-done.2 = f32[1024,1024]{1,0:T(8,128)S(1)} copy-done((f32[1024,1024]{1,0:T(8,128)S(1)}, f32[1024,1024]{1,0:T(8,128)}, u32[]{:S(2)}) %copy-start.2) | copy-done | bytes 4194328
  27.6 1.7 %copy-done.7 = f32[1024,616]{0,1:T(8,128)S(1)} copy-done((f32[1024,616]{0,1:T(8,128)S(1)}, f32[1024,616]{0,1:T(8,128)}, u32[]{:S(2)}) %copy-start.7) | copy-done | bytes 2523160
  29.3 1.4 copy-done.8
  30.8 3.6 %shard_map.124 = (bf16[768,1024]{1,0:T(8,128)(2,1)S(1)}, bf16[768,1024]{1,0:T(8,128)(2,1)S(1)}, bf16[1024,1024]{1,0:T(8,128)(2,1)S(1)}, bf16[1024,1024]{1,0:T(8,...) custom-call(f32[274,1024]{1,0:T(8,128)S(1)} %get-tuple-element.109.w, ...), custom_call_target="tpu_custom_call" | custom-call | tf_op jit(solution)/shard_map/pallas_call | solution.py:59
  34.4 11.6 %shard_map.125 = (f32[512,384]{1,0:T(8,128)S(1)}, f32[512,384]{1,0:T(8,128)S(1)}) custom-call(f32[512,384]{1,0:T(8,128)S(1)} %copy-done.10, f32[512,384]{1,0:T(8,128)} %collective-permute-done.other, bf16[512,1024]{1,0:T(8,128)(2,1)S(1)} %copy-done.3, bf16[512,1024]{1,0:T(8,128)(2,1)S(1)} %copy-done.5, bf16[768,1024]{1,0:T(8,128)(2,1)S(1)} %get-tuple-element.59.rest_0_, ...), custom_call_target="tpu_custom_call" | custom-call | tf_op jit(solution)/shard_map/pallas_call | solution.py:59
  46.5 1.9 %collective-permute-done.1.other = f32[512,384]{1,0:T(8,128)S(1)} collective-permute-done((f32[512,384]{1,0:T(8,128)S(1)}, f32[512,384]{1,0:T(8,128)S(1)}, u32[]{:S(2)}, u32[]{:S(2)}) %collective-permute-start.1) | collective-permute-done | bytes 786464 | tf_op jit(solution)/shard_map/ppermute | solution.py:374
  48.4 3.9 %shard_map.126 = (f32[2048,384]{1,0:T(8,128)S(1)}, f32[32,274]{1,0:T(8,128)S(1)}, f32[32,274]{1,0:T(8,128)S(1)}, f32[64,274]{1,0:T(8,128)S(1)}, f32[64,274]{1,0:T(8,128)S(1)}) custom-call(f32[512,384]{1,0:T(8,128)S(1)} %get-tuple-element.68.own, f32[512,384]{1,0:T(8,128)S(1)} %collective-permute-done.1.other, f32[64,32,4]{2,1,0:T(8,128)S(1)} %copy.27.weights, ...), custom_call_target="tpu_custom_call" | custom-call | tf_op jit(solution)/shard_map/pallas_call | solution.py:59
  52.4 22.0 %shard_map.127 = (f32[32,274]{1,0:T(8,128)S(1)}, f32[32,274]{1,0:T(8,128)S(1)}, f32[64,274]{1,0:T(8,128)S(1)}, f32[64,274]{1,0:T(8,128)S(1)}) custom-call(f32[32,274]{1,0:T(8,128)S(1)} %get-tuple-element.71.first_lat, f32[32,274]{1,0:T(8,128)S(1)} %get-tuple-element.72.last_lat, f32[64,274]{1,0:T(8,128)S(1)} %get-tuple-element.73.first_lon, ...), custom_call_target="tpu_custom_call" | custom-call | tf_op jit(solution)/shard_map/pallas_call | solution.py:59
  74.4 6.0 %shard_map.128 = (f32[64,32,274]{2,1,0:T(8,128)S(1)}, f32[32,274]{1,0:T(8,128)S(1)}, f32[32,274]{1,0:T(8,128)S(1)}, f32[64,274]{1,0:T(8,128)S(1)}, f32[64,274]{1,0:T(8,128)S(1)}, /*index=5*/f32[8,128]{1,0:T(8,128)S(1)}) custom-call(f32[2048,384]{1,0:T(8,128)S(1)} %get-tuple-element.70.spread, f32[32,274]{1,0:T(8,128)S(1)} %get-tuple-element.75.before, ...), custom_call_target="tpu_custom_call" | custom-call | tf_op jit(solution)/shard_map/pallas_call | solution.py:59
  80.4 8.4 %shard_map.129 = (f32[32,274]{1,0:T(8,128)S(1)}, f32[32,274]{1,0:T(8,128)S(1)}, f32[64,274]{1,0:T(8,128)S(1)}, f32[64,274]{1,0:T(8,128)S(1)}) custom-call(f32[32,274]{1,0:T(8,128)S(1)} %get-tuple-element.80.first_lat, f32[32,274]{1,0:T(8,128)S(1)} %get-tuple-element.81.last_lat, f32[64,274]{1,0:T(8,128)S(1)} %get-tuple-element.82.first_lon, ...), custom_call_target="tpu_custom_call" | custom-call | tf_op jit(solution)/shard_map/pallas_call | solution.py:59
  88.8 4.2 %shard_map.130 = (f32[512,384]{1,0:T(8,128)S(1)}, f32[512,384]{1,0:T(8,128)S(1)}) custom-call(f32[64,32,274]{2,1,0:T(8,128)S(1)} %get-tuple-element.79.field.w, f32[32,274]{1,0:T(8,128)S(1)} %get-tuple-element.84.before, f32[32,274]{1,0:T(8,128)S(1)} %get-tuple-element.85.after, f32[64,274]{1,0:T(8,128)S(1)} %get-tuple-element.86.left, ...), custom_call_target="tpu_custom_call" | custom-call | tf_op jit(solution)/shard_map/pallas_call | solution.py:59
  93.1 2.3 %collective-permute-done.2.other = f32[512,384]{1,0:T(8,128)S(1)} collective-permute-done((f32[512,384]{1,0:T(8,128)S(1)}, f32[512,384]{1,0:T(8,128)S(1)}, u32[]{:S(2)}, u32[]{:S(2)}) %collective-permute-start.2) | collective-permute-done | bytes 786464 | tf_op jit(solution)/shard_map/ppermute | solution.py:374
  95.4 10.8 %shard_map.131 = (f32[512,384]{1,0:T(8,128)S(1)}, f32[512,384]{1,0:T(8,128)S(1)}) custom-call(f32[512,384]{1,0:T(8,128)S(1)} %get-tuple-element.88.own, f32[512,384]{1,0:T(8,128)S(1)} %collective-permute-done.2.other, bf16[512,1024]{1,0:T(8,128)(2,1)S(1)} %copy-done.4, bf16[512,1024]{1,0:T(8,128)(2,1)S(1)} %copy-done.6, ...), custom_call_target="tpu_custom_call" | custom-call | tf_op jit(solution)/shard_map/pallas_call | solution.py:59
  106.4 2.2 %collective-permute-done.3.other = f32[512,384]{1,0:T(8,128)S(1)} collective-permute-done((f32[512,384]{1,0:T(8,128)S(1)}, f32[512,384]{1,0:T(8,128)S(1)}, u32[]{:S(2)}, u32[]{:S(2)}) %collective-permute-start.3) | collective-permute-done | bytes 786464 | tf_op jit(solution)/shard_map/ppermute | solution.py:374
  108.6 3.7 %shard_map.132 = (f32[2048,384]{1,0:T(8,128)S(1)}, f32[32,274]{1,0:T(8,128)S(1)}, f32[32,274]{1,0:T(8,128)S(1)}, f32[64,274]{1,0:T(8,128)S(1)}, f32[64,274]{1,0:T(8,128)S(1)}) custom-call(f32[512,384]{1,0:T(8,128)S(1)} %get-tuple-element.90.own, f32[512,384]{1,0:T(8,128)S(1)} %collective-permute-done.3.other, f32[64,32,4]{2,1,0:T(8,128)S(1)} %copy.27.weights, ...), custom_call_target="tpu_custom_call" | custom-call | tf_op jit(solution)/shard_map/pallas_call | solution.py:59
  112.3 23.6 %shard_map.133 = (f32[32,274]{1,0:T(8,128)S(1)}, f32[32,274]{1,0:T(8,128)S(1)}, f32[64,274]{1,0:T(8,128)S(1)}, f32[64,274]{1,0:T(8,128)S(1)}) custom-call(f32[32,274]{1,0:T(8,128)S(1)} %get-tuple-element.93.first_lat, f32[32,274]{1,0:T(8,128)S(1)} %get-tuple-element.94.last_lat, f32[64,274]{1,0:T(8,128)S(1)} %get-tuple-element.95.first_lon, ...), custom_call_target="tpu_custom_call" | custom-call | tf_op jit(solution)/shard_map/pallas_call | solution.py:59
  135.9 6.2 %shard_map.134 = (f32[64,32,274]{2,1,0:T(8,128)S(1)}, f32[8,128]{1,0:T(8,128)S(1)}) custom-call(f32[2048,384]{1,0:T(8,128)S(1)} %get-tuple-element.92.spread, f32[32,274]{1,0:T(8,128)S(1)} %get-tuple-element.97.before, f32[32,274]{1,0:T(8,128)S(1)} %get-tuple-element.98.after, f32[64,274]{1,0:T(8,128)S(1)} %get-tuple-element.99.left, ...), custom_call_target="tpu_custom_call" | custom-call | tf_op jit(solution)/shard_map/pallas_call | solution.py:59
  142.1 10.7 %shard_map.135.sums = f32[8,128]{1,0:T(8,128)S(1)} custom-call(f32[8,128]{1,0:T(8,128)S(1)} %get-tuple-element.102.x_ref), custom_call_target="tpu_custom_call" | custom-call | tf_op jit(solution)/shard_map/pallas_call | solution.py:59
  152.8 4.5 %shard_map.136 = (f32[64,32,274]{2,1,0:T(8,128)}, f32[64,32,274]{2,1,0:T(8,128)}) custom-call(f32[8,128]{1,0:T(8,128)S(1)} %shard_map.135.sums, f32[8,128]{1,0:T(8,128)S(1)} %get-tuple-element.67.rest_8_.scale, f32[64,32,274]{2,1,0:T(8,128)S(1)} %copy-done.1, f32[64,32,274]{2,1,0:T(8,128)S(1)} %get-tuple-element.79.field.w, ...), custom_call_target="tpu_custom_call" | custom-call | tf_op jit(solution)/shard_map/pallas_call | solution.py:363
  (38 shorter events, 5.1 us)
Async XLA Ops:
  0.6 16.8 %copy-start.12 = (s32[32]{0:T(128)S(1)}, s32[32]{0:T(128)}, u32[]{:S(2)}) copy-start(s32[32]{0:T(128)} %counts.7) | copy-start | bytes 388
  0.6 16.8 %copy-start.11 = (s32[2,512]{1,0:T(2,128)S(1)}, s32[2,512]{1,0:T(2,128)}, u32[]{:S(2)}) copy-start(s32[2,512]{1,0:T(2,128)} %cells.7) | copy-start | bytes 12292
  17.4 1.9 %copy-start = (f32[64,32,274]{2,1,0:T(8,128)S(1)}, f32[64,32,274]{2,1,0:T(8,128)}, u32[]{:S(2)}) copy-start(f32[64,32,274]{2,1,0:T(8,128)} %b.1) | copy-start | bytes 6733828
  19.3 6.1 %copy-start.13 = (f32[548,1024]{1,0:T(8,128)S(1)}, f32[548,1024]{1,0:T(8,128)}, u32[]{:S(2)}) copy-start(f32[548,1024]{1,0:T(8,128)} %param.14) | copy-start | bytes 6733828
  24.6 0.9 copy-start.9
  25.4 8.9 %collective-permute-start = (f32[512,384]{1,0:T(8,128)}, f32[512,384]{1,0:T(8,128)}, u32[]{:S(2)}, u32[]{:S(2)}) collective-permute-start(f32[512,384]{1,0:T(8,128)} %get-tuple-element.58), channel_id=1, source_target_pairs={{0,16},{16,0},{1,17},{17,1},{2,18},{18,2},{3,19},{19,3},{4,20},{20... | collective-permute-start | bytes 2359304 | tf_op jit(solution)/shard_map/ppermute | solution.py:374
  25.4 2.2 %copy-start.2 = (f32[1024,1024]{1,0:T(8,128)S(1)}, f32[1024,1024]{1,0:T(8,128)}, u32[]{:S(2)}) copy-start(f32[1024,1024]{1,0:T(8,128)} %w_mid.1) | copy-start | bytes 12582916
  27.6 1.7 %copy-start.7 = (f32[1024,616]{0,1:T(8,128)S(1)}, f32[1024,616]{0,1:T(8,128)}, u32[]{:S(2)}) copy-start(f32[1024,616]{0,1:T(8,128)} %param.16) | copy-start | bytes 7569412
  29.3 1.4 copy-start.8
  30.8 3.6 %copy-start.3 = (bf16[512,1024]{1,0:T(8,128)(2,1)S(1)}, bf16[512,1024]{1,0:T(8,128)(2,1)}, u32[]{:S(2)}) copy-start(bf16[512,1024]{1,0:T(8,128)(2,1)} %gate_one.3) | copy-start | bytes 3145732
  30.8 3.6 %copy-start.5 = (bf16[512,1024]{1,0:T(8,128)(2,1)S(1)}, bf16[512,1024]{1,0:T(8,128)(2,1)}, u32[]{:S(2)}) copy-start(bf16[512,1024]{1,0:T(8,128)(2,1)} %gate_two.3) | copy-start | bytes 3145732
  30.8 3.6 %copy-start.10 = (f32[512,384]{1,0:T(8,128)S(1)}, f32[512,384]{1,0:T(8,128)}, u32[]{:S(2)}) copy-start(f32[512,384]{1,0:T(8,128)} %copy-done.9) | copy-start | bytes 2359300
  34.4 40.0 %copy-start.1 = (f32[64,32,274]{2,1,0:T(8,128)S(1)}, f32[64,32,274]{2,1,0:T(8,128)}, u32[]{:S(2)}) copy-start(f32[64,32,274]{2,1,0:T(8,128)} %b.1) | copy-start | bytes 6733828
  46.0 2.5 %collective-permute-start.1 = (f32[512,384]{1,0:T(8,128)S(1)}, f32[512,384]{1,0:T(8,128)S(1)}, u32[]{:S(2)}, u32[]{:S(2)}) collective-permute-start(f32[512,384]{1,0:T(8,128)S(1)} %get-tuple-element.69), channel_id=1, source_target_pairs={{0,16},{16,0},{1,17},{17,1},{2,18},{18,2},{3,19},{19,3},{4,20},{20... | collective-permute-start | bytes 2359304 | tf_op jit(solution)/shard_map/ppermute | solution.py:374
  88.8 6.6 %copy-start.4 = (bf16[512,1024]{1,0:T(8,128)(2,1)S(1)}, bf16[512,1024]{1,0:T(8,128)(2,1)}, u32[]{:S(2)}) copy-start(bf16[512,1024]{1,0:T(8,128)(2,1)} %gate_one.3) | copy-start | bytes 3145732
  88.8 6.6 %copy-start.6 = (bf16[512,1024]{1,0:T(8,128)(2,1)S(1)}, bf16[512,1024]{1,0:T(8,128)(2,1)}, u32[]{:S(2)}) copy-start(bf16[512,1024]{1,0:T(8,128)(2,1)} %gate_two.3) | copy-start | bytes 3145732
  93.1 2.4 %collective-permute-start.2 = (f32[512,384]{1,0:T(8,128)S(1)}, f32[512,384]{1,0:T(8,128)S(1)}, u32[]{:S(2)}, u32[]{:S(2)}) collective-permute-start(f32[512,384]{1,0:T(8,128)S(1)} %get-tuple-element.89), channel_id=1, source_target_pairs={{0,16},{16,0},{1,17},{17,1},{2,18},{18,2},{3,19},{19,3},{4,20},{20... | collective-permute-start | bytes 2359304 | tf_op jit(solution)/shard_map/ppermute | solution.py:374
  106.2 2.4 %collective-permute-start.3 = (f32[512,384]{1,0:T(8,128)S(1)}, f32[512,384]{1,0:T(8,128)S(1)}, u32[]{:S(2)}, u32[]{:S(2)}) collective-permute-start(f32[512,384]{1,0:T(8,128)S(1)} %get-tuple-element.91), channel_id=1, source_target_pairs={{0,16},{16,0},{1,17},{17,1},{2,18},{18,2},{3,19},{19,3},{4,20},{20... | collective-permute-start | bytes 2359304 | tf_op jit(solution)/shard_map/ppermute | solution.py:374
